TPU v7x, 256 devices: a whole 4x4x8 slice. The times are simulated.
256 devices in a mesh: replica: 16 (over x, y), tensor: 16 (over z, core).
Axes of the slice: x: 4, y: 4, z: 8, core: 2. Of those that a mesh axis runs over, the one named last changes fastest.
Arguments:
- momentum: float32 [16, 1024, 8192], P('replica', None, 'tensor'), may hold values from -6 to 6
- gradient: bfloat16 [16, 1024, 8192], P('replica', None, 'tensor'), may hold values from -110 to 110
- kept_freq: int32 [16, 16, 128, 32], P('replica', None, 'tensor'), may hold values from 0 to 4095, all different within a row
- clip_flag: int32 [16], P('replica'), may hold values from 0 to 1
Outputs:
- new_momentum: float32 [16, 1024, 8192], P('replica', None, 'tensor')
- update: float32 [1024, 8192], P(None, 'tensor')
Inputs may be any that keep to these rules, and one draw needn't show every extreme that they name: `kept_freq`: within one block the 32 frequencies of a replica differ.
All inputs are finite; a program needn't handle non-finite values.
Results may differ from a plain program's by a relative error of at most 0.0003.
Values sent between devices are 32-bit elements; how exact they have to be, the bound alone decides.
No kernel may reach another device: no remote copies, remote signals or barrier semaphores. Data moves between devices by JAX's collectives and lax.ppermute only.
A program may use at most 64 MiB of HBM per device.

v0:
```python
import math

import jax
import jax.numpy as jnp
from jax import lax
from jax.sharding import PartitionSpec as P

GROUP = 64


CLIP_RMS = 0.5
DECAY = 0.9


def cosine_table(width):
    freq = jnp.arange(width, dtype=jnp.float32)[:, None]
    place = jnp.arange(width, dtype=jnp.float32)[None, :]
    weight = jnp.where(freq == 0, 1.0, 2.0) / width
    return jnp.sqrt(weight) * jnp.cos(math.pi * (2.0 * place + 1.0) * freq / (2.0 * width))


def forward(field, table):
    width = table.shape[0]
    blocks = field.reshape(field.shape[0] // width, width, field.shape[1] // width, width)
    rows_done = jnp.einsum("ap,ipjq->iajq", table, blocks, precision=lax.Precision.HIGHEST)
    return jnp.einsum("bq,iajq->ijab", table, rows_done, precision=lax.Precision.HIGHEST)


def inverse(coef, table):
    width = table.shape[0]
    rows_done = jnp.einsum("ap,ijab->ipjb", table, coef, precision=lax.Precision.HIGHEST)
    full = jnp.einsum("bq,ipjb->ipjq", table, rows_done, precision=lax.Precision.HIGHEST)
    return full.reshape(coef.shape[0] * width, coef.shape[1] * width)


def spread_into(base, values, freq):
    brows, bcols = (freq.shape[-3], freq.shape[-2])
    row_ids = jnp.arange(brows, dtype=jnp.int32)[:, None, None]
    col_ids = jnp.arange(bcols, dtype=jnp.int32)[None, :, None]
    return base.at[row_ids, col_ids, freq].add(values)


def body(momentum, gradient, kept_freq, clip_flag):
    table = cosine_table(GROUP)
    cells = GROUP * GROUP
    replicas = lax.axis_size("replica")
    mom = momentum[0]
    grad = gradient[0].astype(jnp.float32)
    count = replicas * lax.axis_size("tensor") * mom.shape[0] * mom.shape[1]
    total = lax.psum(jnp.sum(grad * grad), ("replica", "tensor"))
    rms = jnp.sqrt(total / count)
    factor = jnp.minimum(jnp.float32(1.0), CLIP_RMS / (rms + 1e-06))
    scale = jnp.where(clip_flag[0] == 1, factor, jnp.float32(1.0))
    accum = DECAY * mom + scale * grad
    coef = forward(accum, table)
    brows, bcols = (coef.shape[0], coef.shape[1])
    own_freq = kept_freq[0]
    flat = coef.reshape(brows, bcols, cells)
    kept = jnp.take_along_axis(flat, own_freq, axis=2)
    empty = jnp.zeros((brows, bcols, cells), jnp.float32)
    sparse = spread_into(empty, kept, own_freq)
    new_mom = accum - inverse(sparse.reshape(coef.shape), table)
    pooled = lax.psum(sparse, "replica")
    update = inverse((pooled / replicas).reshape(coef.shape), table)
    return (new_mom[None], update)


def solution(mesh):
    placed = (
        P("replica", None, "tensor"),
        P("replica", None, "tensor"),
        P("replica", None, "tensor", None),
        P("replica"),
    )
    return jax.shard_map(
        body,
        mesh=mesh,
        in_specs=placed,
        out_specs=(P("replica", None, "tensor"), P(None, "tensor")),
        check_vma=False,
    )
```

profile of v0, /device:TPU:1, one launch (start us, length us, event | category | flops | bytes accessed | tf_op | source)
XLA Modules:
  0.0 297.4 jit_solution(893280245130584605)
XLA Ops:
  7.2 0.0 copy-start.2
  7.2 0.0 all-reduce.2.cloned.1.call-start
  7.2 2.4 fusion.11
  10.3 81.4 %psum.14 = f32[]{:T(128)} all-reduce(f32[]{:T(128)} %fusion.11), channel_id=1, replica_groups=mesh['replica'=16,'tensor'=16] {'replica','tensor'}, use_global_device_ids=true, to_apply=%region_1.2 | all-reduce | flops 1 | bytes 8 | tf_op jit(solution)/shard_map/psum | solution.py:50
  92.4 0.9 shift-left_or_fusion
  93.3 0.1 reshape.105
  93.4 0.8 and_reduce_fusion
  94.2 0.8 multiply_reduce_fusion
  95.0 0.1 reshape.111
  95.1 0.0 copy-done.2
  95.1 2.0 fusion.12
  97.1 0.0 copy-start
  97.1 2.7 add.67
  99.7 0.0 copy-done
  99.8 6.7 %fusion.6 = f32[16,8,64,64]{2,3,1,0:T(8,128)S(1)} fusion(f32[16,64,8,64]{3,2,1,0:T(8,128)} %add.67, f32[64]{0:T(128)S(1)} %get-tuple-element.5, f32[64]{0:T(128)S(1)} %get-tuple-element.4), kind=kOutput, calls=%fused_computation.8 | convolution fusion | flops 402665472 | bytes 4194816 | tf_op jit(solution)/shard_map/ap,ipjq->iajq/dot_general | solution.py:25
  106.5 5.2 %fusion.8 = f32[16,8,64,64]{3,2,1,0:T(8,128)} fusion(f32[16,8,64,64]{2,3,1,0:T(8,128)S(1)} %fusion.6, f32[64]{0:T(128)S(1)} %get-tuple-element.5, f32[64]{0:T(128)S(1)} %get-tuple-element.4), kind=kOutput, calls=%fused_computation.12 | convolution fusion | flops 402665472 | bytes 4194816 | tf_op jit(solution)/shard_map/bq,iajq->ijab/dot_general | solution.py:26
  111.7 3.5 %reshape.95 = f32[16,8,4096]{2,1,0:T(8,128)S(1)} reshape(f32[16,8,64,64]{3,2,1,0:T(8,128)} %fusion.8) | data formatting | bytes 4194304 | tf_op jit(solution)/shard_map/reshape | solution.py:58
  115.2 0.0 copy-start.3
  115.2 32.0 %gather_fusion = f32[4096]{0:T(1024)S(1)} fusion(f32[16,8,4096]{2,1,0:T(8,128)S(1)} %reshape.95, s32[4096]{0:T(1024)S(1)} %reshape.105), kind=kCustom, calls=%fused_computation | custom fusion | bytes 81920 | tf_op jit(solution)/shard_map/jit(take_along_axis)/gather | solution.py:59
  147.2 0.1 reshape.108
  147.3 0.0 copy-done.3
  147.3 0.1 reshape.113
  147.4 22.6 %scatter_custom_fusion = f32[524288]{0:T(1024)S(1)} fusion(s32[4096]{0:T(1024)S(1)} %reshape.111, f32[4096]{0:T(1024)S(1)} %reshape.113, f32[]{:T(128)} %constant.19.clone.1), kind=kCustom, calls=%fused_computation.15 | custom fusion | flops 4096 | bytes 2097156
  170.0 1.6 reshape.103
  171.6 0.0 all-reduce.2.cloned.1.call-update
  171.6 2.3 reshape.96
  173.9 5.9 %fusion.19 = f32[16,8,64,64]{2,3,1,0:T(8,128)S(1)} fusion(f32[16,8,64,64]{3,2,1,0:T(8,128)} %reshape.96, f32[64]{0:T(128)S(1)} %get-tuple-element.5, f32[64]{0:T(128)S(1)} %get-tuple-element.4), kind=kOutput, calls=%fused_computation.29 | convolution fusion | flops 402665472 | bytes 4194816 | tf_op jit(solution)/shard_map/ap,ijab->ipjb/dot_general | solution.py:31
  179.7 3.5 %fusion.2 = f32[16,64,8,64]{3,1,2,0:T(8,128)S(1)} fusion(f32[16,8,64,64]{2,3,1,0:T(8,128)S(1)} %fusion.19, f32[64]{0:T(128)S(1)} %get-tuple-element.5, f32[64]{0:T(128)S(1)} %get-tuple-element.4), kind=kOutput, calls=%fused_computation.4 | convolution fusion | flops 402665472 | bytes 4194816 | tf_op jit(solution)/shard_map/bq,ipjb->ipjq/dot_general | solution.py:32
  183.3 5.2 %copy.6 = f32[16,64,8,64]{3,2,1,0:T(8,128)} copy(f32[16,64,8,64]{3,1,2,0:T(8,128)S(1)} %fusion.2) | data formatting | bytes 4194304 | tf_op jit(solution)/shard_map/bq,ipjb->ipjq/dot_general | solution.py:32
  188.5 0.0 copy-start.1
  188.5 5.0 %reshape.97 = f32[1,1024,512]{2,1,0:T(8,128)} reshape(f32[16,64,8,64]{3,2,1,0:T(8,128)} %copy.6) | data formatting | bytes 4194304 | tf_op jit(solution)/shard_map/reshape | solution.py:33
  193.5 0.0 copy-done.1
  193.5 3.4 %sub.4 = f32[1,1024,512]{2,1,0:T(8,128)} subtract(f32[1,1024,512]{2,1,0:T(8,128)S(1)} %copy-done.1, f32[1,1024,512]{2,1,0:T(8,128)} %reshape.97) | non-fusion elementwise | flops 524288 | bytes 6291456 | tf_op jit(solution)/shard_map/sub | solution.py:62
  196.8 69.4 %all-reduce.2.cloned.1.call-done = f32[16,8,4096]{2,1,0:T(8,128)} async-done(((f32[16,8,4096]{2,1,0:T(8,128)}), f32[16,8,4096]{2,1,0:T(8,128)}) %all-reduce.2.cloned.1.call-update) | async-done | bytes 2097168 | tf_op jit(solution)/shard_map/psum | solution.py:63
  266.2 1.8 broadcast_multiply_fusion
  268.0 3.2 %reshape.98 = f32[16,8,64,64]{3,2,1,0:T(8,128)} reshape(f32[16,8,4096]{2,1,0:T(8,128)S(1)} %broadcast_multiply_fusion) | data formatting | bytes 4194304 | tf_op jit(solution)/shard_map/reshape | solution.py:64
  271.2 5.9 %fusion.16 = f32[16,8,64,64]{2,3,1,0:T(8,128)S(1)} fusion(f32[16,8,64,64]{3,2,1,0:T(8,128)} %reshape.98, f32[64]{0:T(128)S(1)} %get-tuple-element.5, f32[64]{0:T(128)S(1)} %get-tuple-element.4), kind=kOutput, calls=%fused_computation.26 | convolution fusion | flops 402665472 | bytes 4194816 | tf_op jit(solution)/shard_map/ap,ijab->ipjb/dot_general | solution.py:31
  277.1 3.5 %fusion = f32[16,64,8,64]{3,1,2,0:T(8,128)S(1)} fusion(f32[16,8,64,64]{2,3,1,0:T(8,128)S(1)} %fusion.16, f32[64]{0:T(128)S(1)} %get-tuple-element.5, f32[64]{0:T(128)S(1)} %get-tuple-element.4), kind=kOutput, calls=%fused_computation.2 | convolution fusion | flops 402665472 | bytes 4194816 | tf_op jit(solution)/shard_map/bq,ipjb->ipjq/dot_general | solution.py:32
  280.6 5.2 %copy.7 = f32[16,64,8,64]{3,2,1,0:T(8,128)} copy(f32[16,64,8,64]{3,1,2,0:T(8,128)S(1)} %fusion) | data formatting | bytes 4194304 | tf_op jit(solution)/shard_map/bq,ipjb->ipjq/dot_general | solution.py:32
  285.8 4.8 %reshape.99 = f32[1024,512]{1,0:T(8,128)} reshape(f32[16,64,8,64]{3,2,1,0:T(8,128)} %copy.7) | data formatting | bytes 4194304 | tf_op jit(solution)/shard_map/reshape | solution.py:33
  (5 shorter events, 0.1 us)
Async XLA Ops:
  7.2 87.9 %copy-start.2 = (bf16[1,1024,512]{2,1,0:T(8,128)(2,1)S(1)}, bf16[1,1024,512]{2,1,0:T(8,128)(2,1)}, u32[]{:S(2)}) copy-start(bf16[1,1024,512]{2,1,0:T(8,128)(2,1)} %param.5) | copy-start | bytes 3145732
  7.2 259.0 %all-reduce.2.cloned.1.call-start = ((), (), s32[]{:S(2)}) async-start(), calls=%async_computation | async-start | bytes 4194304 | tf_op jit(solution)/shard_map/psum | solution.py:63
  97.1 2.7 copy-start
  115.2 32.1 %copy-start.3 = (s32[1,16,8,32]{3,2,1,0:T(8,128)S(1)}, s32[1,16,8,32]{3,2,1,0:T(8,128)}, u32[]{:S(2)}) copy-start(s32[1,16,8,32]{3,2,1,0:T(8,128)} %param.6) | copy-start | bytes 49156
  188.5 5.0 %copy-start.1 = (f32[1,1024,512]{2,1,0:T(8,128)S(1)}, f32[1,1024,512]{2,1,0:T(8,128)}, u32[]{:S(2)}) copy-start(f32[1,1024,512]{2,1,0:T(8,128)} %copy-done) | copy-start | bytes 6291460
Sparse Core Ops, SparseCore 0:
  171.7 94.4 all-reduce.1
where the time goes:
time: 298 us; the launch traced here: 297 us
  blocking collectives  81.4 us (27%)
  waiting for transfers between devices  69.4 us (23%)
  local copies, waits for them, and re-layouts  65.7 us (22%)
  other arithmetic  34.6 us (12%)
  matrix products  30.7 us (10%)
  between operations  15.6 us (5%)
    psum x1, blocking collectives, body(): total = lax.psum(jnp.sum(grad * grad), ('replica', 'tensor'))  81.4 us
    psum x1, waiting for transfers between devices, body(): pooled = lax.psum(sparse, 'replica')  69.4 us
    gather x2, local copies, waits for them, and re-layouts, body(): kept = jnp.take_along_axis(flat, own_freq, axis=2)  32 us
    unnamed x4, other arithmetic  24.1 us
    dot_general x2, matrix products, inverse(): jnp.einsum('ap,ijab->ipjb', table, coef, precision=lax.Precision.HIGHEST)  11.7 us
    dot_general x2, local copies, waits for them, and re-layouts, inverse(): jnp.einsum('bq,ipjb->ipjq', table, rows_done, precision=lax.Precision.HIG...  10.4 us
    reshape x2, local copies, waits for them, and re-layouts, inverse(): return full.reshape(coef.shape[0] * width, coef.shape[1] * width)  9.74 us
    dot_general x2, matrix products, inverse(): jnp.einsum('bq,ipjb->ipjq', table, rows_done, precision=lax.Precision.HIG...  7.07 us
  transfers between devices with their start and end apart: 1, of which 1 were waited for; matrix products, arithmetic and copies ran while one was open for 8% of the time, Pallas kernels for 0%

commit v1 on v0

v1 whole, which is shorter than its diff:
```python
import math

import jax
import jax.numpy as jnp
import ml_dtypes
import numpy as np
from jax import lax
from jax.experimental import pallas as pl
from jax.experimental.pallas import tpu as pltpu
from jax.sharding import PartitionSpec as P

GROUP = 64
TOPK = 32
LANES = 128
CLIP_RMS = 0.5
DECAY = 0.9
F32 = jnp.float32
BF16 = jnp.bfloat16


def split_table(table):
    high = table.astype(ml_dtypes.bfloat16)
    low = (table - high.astype(np.float64)).astype(ml_dtypes.bfloat16)
    return high, low


def tables():
    freq = np.arange(GROUP)[:, None]
    place = np.arange(GROUP)[None, :]
    table = np.sqrt(np.where(freq == 0, 1.0, 2.0) / GROUP) * np.cos(math.pi * (2 * place + 1) * freq / (2 * GROUP))
    high, low = split_table(table)
    stacked = np.concatenate([high.T, low.T], axis=0)
    eye = np.eye(4)
    rows = np.stack(split_table(np.kron(eye, table.T)))
    cols = np.stack(split_table(np.kron(eye, table)))
    return stacked, rows, cols


def halves(x):
    high = x.astype(BF16)
    return high, (x - high.astype(F32)).astype(BF16)


def dot(a, b):
    return jnp.dot(a, b, preferred_element_type=F32)


def dot_nt(a, b):
    return lax.dot_general(a, b, (((1,), (1,)), ((), ())), preferred_element_type=F32)


def square_kernel(grad_ref, out_ref):
    @pl.when(pl.program_id(0) == 0)
    def _():
        out_ref[...] = jnp.zeros_like(out_ref)

    g = grad_ref[...].astype(F32)
    g = g * g
    g = g.reshape(-1, 8, g.shape[1]).sum(axis=0)
    part = sum(g[:, n * LANES:(n + 1) * LANES] for n in range(g.shape[1] // LANES))
    for n in range(out_ref.shape[0]):
        out_ref[n] += part


def table_rows(freq, stacked):
    a = lax.shift_right_logical(freq, 6)
    b = lax.bitwise_and(freq, GROUP - 1)
    place = lax.broadcasted_iota(jnp.int32, (GROUP, LANES), 0)
    hot_a = jnp.where(place == a, 1.0, 0.0).astype(BF16)
    hot_b = jnp.where(place == b, 1.0, 0.0).astype(BF16)
    both = dot(stacked, jnp.concatenate([hot_a, hot_b], axis=1))
    return both[:GROUP, :LANES], both[GROUP:, :LANES], both[:GROUP, LANES:], both[GROUP:, LANES:]


def diagonal(x):
    lane = lax.broadcasted_iota(jnp.int32, x.shape, 1)
    zero = jnp.zeros_like(x)
    return jnp.concatenate([jnp.where(lane // TOPK == m, x, zero) for m in range(4)], axis=0)


def kept_kernel(flag_ref, mom_ref, grad_ref, freq_ref, square_ref, stacked_ref, out_ref):
    step = pl.program_id(0)
    flag = (flag_ref[0] == 1).astype(F32)
    stacked = stacked_ref[...]
    copies = out_ref.shape[0]
    chunks = freq_ref.shape[0]
    freqs = freq_ref[pl.ds(pl.multiple_of(step * 8, 8), 8), :]
    us, vs = [], []
    for s in range(8):
        row, col = s // 2, s % 2
        freq = freqs[s:s + 1, :]
        ah, al, bh, bl = table_rows(freq, stacked)
        weights = jnp.concatenate([diagonal(bh), diagonal(bl)], axis=1).astype(BF16)
        x = mom_ref[row * GROUP:(row + 1) * GROUP, col * 256:(col + 1) * 256]
        g = grad_ref[row * GROUP:(row + 1) * GROUP, col * 256:(col + 1) * 256]
        xh, xl = halves(x)
        y = dot(jnp.concatenate([xh, xl, g], axis=0), weights)
        y = y[:, :LANES] + y[:, LANES:]
        a = ah + al
        km = jnp.sum((y[:GROUP] + y[GROUP:2 * GROUP]) * a, axis=0, keepdims=True)
        kg = jnp.sum(y[2 * GROUP:] * a, axis=0, keepdims=True)
        us.append(DECAY * km + (1.0 - flag) * kg)
        vs.append(flag * kg)
    u = jnp.concatenate(us, axis=0)
    v = jnp.concatenate(vs, axis=0)
    f = freqs.astype(F32)
    at = pl.multiple_of(step * 8, 8)
    for n in range(copies):
        out_ref[n, pl.ds(at, 8), :] = u
        out_ref[n, pl.ds(chunks + at, 8), :] = v
        out_ref[n, pl.ds(2 * chunks + at, 8), :] = f

    @pl.when(step == 0)
    def _():
        total = jnp.sum(square_ref[...], axis=0)
        for n in range(copies):
            out_ref[n, 3 * chunks:, :] = total


def update_kernel(count, flag_ref, mom_ref, grad_ref, own_ref, all_ref, stacked_ref, rows_ref, cols_ref, mom_out, update_out,
                  lists_a, lists_b, lists_h, lists_l, pooled):
    step = pl.program_id(0)
    replicas = all_ref.shape[0]
    chunks = (all_ref.shape[1] - 8) // 3
    stacked = stacked_ref[...]
    total = jnp.sum(all_ref[:, 3 * chunks:, :], axis=0)
    total = jnp.sum(total, axis=(0, 1), keepdims=True)
    rms = jnp.sqrt(total * (1.0 / count))
    factor = jnp.minimum(jnp.float32(1.0), CLIP_RMS / (rms + 1e-06))
    flag = (flag_ref[0] == 1).astype(F32)
    scale = flag * factor + (1.0 - flag)
    at = pl.multiple_of(step * 8, 8)

    lane = lax.broadcasted_iota(jnp.int32, (8, LANES), 1) // TOPK
    for group in range(replicas // 4):
        ks, fs = [], []
        for r in range(4 * group, 4 * group + 4):
            u = all_ref[r, pl.ds(at, 8), :]
            v = all_ref[r, pl.ds(chunks + at, 8), :]
            ks.append((u + factor * v) * (1.0 / replicas))
            fs.append(all_ref[r, pl.ds(2 * chunks + at, 8), :])
        for m in range(4):
            def regroup(xs):
                out = xs[m]
                parts = [x if r == m else pltpu.roll(x, (TOPK * (r - m)) % LANES, 1) for r, x in enumerate(xs)]
                out = parts[0]
                for r in range(1, 4):
                    out = jnp.where(lane == r, parts[r], out)
                return out
            k = regroup(ks)
            f = regroup(fs).astype(jnp.int32)
            high = k.astype(BF16).astype(F32)
            place = slice(group * LANES, (group + 1) * LANES)
            lists_a[m, :, place] = lax.shift_right_logical(f, 6)
            lists_b[m, :, place] = lax.bitwise_and(f, GROUP - 1)
            lists_h[m, :, place] = high
            lists_l[m, :, place] = k - high

    items = replicas * TOPK
    place = lax.broadcasted_iota(jnp.int32, (GROUP, items), 0)
    left = lax.broadcasted_iota(jnp.int32, (GROUP, LANES), 1) < GROUP

    def scatter(s, m):
        here = pl.ds(s, 1)
        hot_a = jnp.where(place == lists_a[m, here, :], 1.0, 0.0).astype(BF16)
        hit = place == lists_b[m, here, :]
        high = jnp.where(hit, lists_h[m, here, :], 0.0).astype(BF16)
        low = jnp.where(hit, lists_l[m, here, :], 0.0).astype(BF16)
        out = dot_nt(hot_a, jnp.concatenate([high, low], axis=0))
        return out + pltpu.roll(out, GROUP, 1)

    def block_row(row, carry):
        top = pl.ds(pl.multiple_of(row * GROUP, GROUP), GROUP)
        for col in range(2):
            s = row * 2 + col
            for pair in range(2):
                both = jnp.where(left, scatter(s, 2 * pair), scatter(s, 2 * pair + 1))
                pooled[top, col * 256 + pair * LANES:col * 256 + (pair + 1) * LANES] = both
            here = pl.ds(at + s, 1)
            freq = own_ref[pl.ds(2 * chunks + at + s, 1), :].astype(jnp.int32)
            k = own_ref[here, :] + factor * own_ref[pl.ds(chunks + at + s, 1), :]
            ah, al, bh, bl = table_rows(freq, stacked)
            wh, wl = halves((bh + bl) * k)
            wh, wl = diagonal(wh.astype(F32)).astype(BF16), diagonal(wl.astype(F32)).astype(BF16)
            ah, al = ah.astype(BF16), al.astype(BF16)
            out = dot_nt(jnp.concatenate([ah, al], axis=1), jnp.concatenate([wh, wh], axis=1)) + dot_nt(ah, wl)
            wide = slice(col * 256, (col + 1) * 256)
            mom_out[top, wide] = DECAY * mom_ref[top, wide] + scale * grad_ref[top, wide].astype(F32) - out
        return carry

    lax.fori_loop(0, 4, block_row, 0)

    ph, plow = halves(pooled[...])
    rh, rl = rows_ref[0], rows_ref[1]
    y = dot(rh, ph) + dot(rh, plow) + dot(rl, ph)
    ch, cl = cols_ref[0], cols_ref[1]
    for col in range(2):
        wide = slice(col * 256, (col + 1) * 256)
        yh, yl = halves(y[:, wide])
        update_out[:, wide] = dot(yh, ch) + dot(yl, ch) + dot(yh, cl)


def full(shape):
    return pl.BlockSpec(shape, lambda i: (0,) * len(shape))


def body(momentum, gradient, kept_freq, clip_flag):
    replicas, tensors = lax.axis_size("replica"), lax.axis_size("tensor")
    mom, grad = momentum[0], gradient[0]
    rows, cols = mom.shape
    steps = rows // 256
    chunks = rows // GROUP * cols // GROUP * TOPK // LANES
    stacked, row_table, col_table = (jnp.asarray(t) for t in tables())
    freq = kept_freq[0].reshape(chunks, LANES)
    band = pl.BlockSpec((256, cols), lambda i: (i, 0))
    scalar = pl.BlockSpec(memory_space=pltpu.SMEM)
    limit = pltpu.CompilerParams(vmem_limit_bytes=40 * 1024 * 1024)

    squares = pl.pallas_call(
        square_kernel,
        grid=(steps,),
        in_specs=[band],
        out_specs=full((tensors, 8, LANES)),
        out_shape=jax.ShapeDtypeStruct((tensors, 8, LANES), F32),
        compiler_params=limit,
    )(grad)
    squares = lax.all_to_all(squares, "tensor", 0, 0)

    message = pl.pallas_call(
        kept_kernel,
        grid=(steps,),
        in_specs=[scalar, band, band, full(freq.shape), full(squares.shape), full(stacked.shape)],
        out_specs=full((replicas, 3 * chunks + 8, LANES)),
        out_shape=jax.ShapeDtypeStruct((replicas, 3 * chunks + 8, LANES), F32),
        compiler_params=limit,
    )(clip_flag, mom, grad, freq, squares, stacked)
    own = message[0]
    everyone = lax.all_to_all(message, "replica", 0, 0)

    new_mom, update = pl.pallas_call(
        lambda *refs: update_kernel(replicas * tensors * rows * cols, *refs),
        grid=(steps,),
        in_specs=[scalar, band, band, full(own.shape), full(everyone.shape), full(stacked.shape),
                  full(row_table.shape), full(col_table.shape)],
        out_specs=[band, band],
        out_shape=[jax.ShapeDtypeStruct((rows, cols), F32)] * 2,
        scratch_shapes=[pltpu.VMEM((4, 8, replicas * TOPK), t) for t in (jnp.int32, jnp.int32, F32, F32)]
        + [pltpu.VMEM((256, cols), F32)],
        compiler_params=limit,
    )(clip_flag, mom, grad, own, everyone, stacked, row_table, col_table)
    return (new_mom[None], update)


def solution(mesh):
    placed = (
        P("replica", None, "tensor"),
        P("replica", None, "tensor"),
        P("replica", None, "tensor", None),
        P("replica"),
    )
    return jax.shard_map(
        body,
        mesh=mesh,
        in_specs=placed,
        out_specs=(P("replica", None, "tensor"), P(None, "tensor")),
        check_vma=False,
    )
```

time: 298 us -> 72.6 us (0.24)
  blocking collectives: 81.4 us -> 0 us
  local copies, waits for them, and re-layouts: 65.7 us -> 8.38 us
  waiting for transfers between devices: 69.4 us -> 18.8 us
  other arithmetic: 34.6 us -> 0 us
  matrix products: 30.7 us -> 0 us
  Pallas kernels: 0 us -> 26.2 us
  starting transfers between devices: 0.04 us -> 16.8 us
  between operations: 15.6 us -> 1.35 us
    psum x1 -> x0, blocking collectives: 81.4 us -> none  [body(): total = lax.psum(jnp.sum(grad * grad), ('replica', 'tensor'))]
    psum x1 -> x0, waiting for transfers between devices: 69.4 us -> none  [body(): pooled = lax.psum(sparse, 'replica')]
    gather x2 -> x0, local copies, waits for them, and re-layouts: 32 us -> none  [body(): kept = jnp.take_along_axis(flat, own_freq, axis=2)]
    dot_general x6 -> x0, matrix products: 30.7 us -> none  [the longest x2 11.7 us: inverse(): jnp.einsum('ap,ijab->ipjb', table, coef, precision=lax.Precision.HIGHEST)]
    pallas_call x0 -> x3, Pallas kernels: none -> 26.2 us  [the longest x1 20.9 us: body(): pl.pallas_call(lambda *refs: update_kernel(replicas * tensors * rows * co...]
    unnamed x4 -> x0, other arithmetic: 24.1 us -> none
    all_to_all x0 -> x2, waiting for transfers between devices: none -> 18.8 us  [the longest x1 12.5 us: body(): everyone = lax.all_to_all(message, 'replica', 0, 0)]
    reshape x5 -> x0, local copies, waits for them, and re-layouts: 18.8 us -> none  [the longest x2 9.74 us: inverse(): return full.reshape(coef.shape[0] * width, coef.shape[1] * width)]
  transfers between devices with their start and end apart: 1 -> 2, of which waited for: 1 -> 2; matrix products, arithmetic and copies ran while one was open for 8% -> 2% of each run, Pallas kernels for 0% -> 0%
where the time goes in v1:
time: 72.6 us; the launch traced here: 71.5 us
  Pallas kernels  26.2 us (36%)
  waiting for transfers between devices  18.8 us (26%)
  starting transfers between devices  16.8 us (23%)
  local copies, waits for them, and re-layouts  8.38 us (12%)
  between operations  1.35 us (2%)
    pallas_call x1, Pallas kernels, body(): pl.pallas_call(lambda *refs: update_kernel(replicas * tensors * rows * co...  20.9 us
    all_to_all x1, waiting for transfers between devices, body(): everyone = lax.all_to_all(message, 'replica', 0, 0)  12.5 us
    all_to_all x1, starting transfers between devices, body(): squares = lax.all_to_all(squares, 'tensor', 0, 0)  9.98 us
    all_to_all x1, starting transfers between devices, body(): everyone = lax.all_to_all(message, 'replica', 0, 0)  6.8 us
    unnamed x20, local copies, waits for them, and re-layouts  6.65 us
    all_to_all x1, waiting for transfers between devices, body(): squares = lax.all_to_all(squares, 'tensor', 0, 0)  6.23 us
    pallas_call x1, Pallas kernels, body(): pl.pallas_call(kept_kernel, grid=(steps,), in_specs=[scalar, band, band,...  4.57 us
  transfers between devices with their start and end apart: 2, of which 2 were waited for; matrix products, arithmetic and copies ran while one was open for 2% of the time, Pallas kernels for 0%

profile of v1, /device:TPU:1, one launch (start us, length us, event | category | flops | bytes accessed | tf_op | source)
XLA Modules:
  0.0 71.5 jit_solution(3897107620232994499)
XLA Ops:
  0.6 0.0 copy-start
  0.6 1.2 %copy-done = bf16[1,1024,512]{2,1,0:T(8,128)(2,1)S(1)} copy-done((bf16[1,1024,512]{2,1,0:T(8,128)(2,1)S(1)}, bf16[1,1024,512]{2,1,0:T(8,128)(2,1)}, u32[]{:S(2)}) %copy-start) | copy-done | bytes 1048600
  1.9 0.8 %shard_map.86 = f32[16,8,128]{2,1,0:T(8,128)} custom-call(bf16[1024,512]{1,0:T(8,128)(2,1)S(1)} %bitcast.7), custom_call_target="tpu_custom_call" | custom-call | tf_op jit(solution)/shard_map/pallas_call | solution.py:219
  2.6 10.0 %all-to-all-start = ((f32[16,8,128]{2,1,0:T(8,128)}), f32[16,8,128]{2,1,0:T(8,128)S(1)}, u32[]{:S(2)}, u32[]{:S(2)}) async-start(f32[16,8,128]{2,1,0:T(8,128)} %shard_map.86), calls=%async_computation | async-start | bytes 131072 | tf_op jit(solution)/shard_map/all_to_all | solution.py:227
  13.3 0.9 %reshape_squeeze.3.freq_ref = s32[32,128]{1,0:T(8,128)S(1)} reshape(s32[1,16,8,32]{3,2,1,0:T(8,128)} %param.9) | data formatting | bytes 32768 | tf_op jit(solution)/shard_map/reshape;squeeze | solution.py:214
  14.2 6.2 %all-to-all-done.square_ref = f32[16,8,128]{2,1,0:T(8,128)S(1)} async-done(((f32[16,8,128]{2,1,0:T(8,128)}), f32[16,8,128]{2,1,0:T(8,128)S(1)}, u32[]{:S(2)}, u32[]{:S(2)}) %all-to-all-start) | async-done | bytes 65568 | tf_op jit(solution)/shard_map/all_to_all | solution.py:227
  20.4 0.0 copy-start.1
  20.4 1.2 %copy-done.1 = bf16[1,1024,512]{2,1,0:T(8,128)(2,1)S(1)} copy-done((bf16[1,1024,512]{2,1,0:T(8,128)(2,1)S(1)}, bf16[1,1024,512]{2,1,0:T(8,128)(2,1)}, u32[]{:S(2)}) %copy-start.1) | copy-done | bytes 1048600
  21.7 0.0 copy-start.3
  21.7 1.6 %copy-done.3 = f32[1,1024,512]{2,1,0:T(8,128)S(1)} copy-done((f32[1,1024,512]{2,1,0:T(8,128)S(1)}, f32[1,1024,512]{2,1,0:T(8,128)}, u32[]{:S(2)}) %copy-start.3) | copy-done | bytes 2097176
  23.2 0.0 copy-start.8
  23.2 0.8 %copy-done.8 = bf16[128,64]{1,0:T(8,128)(2,1)S(1)} copy-done((bf16[128,64]{1,0:T(8,128)(2,1)S(1)}, bf16[128,64]{1,0:T(8,128)(2,1)}, u32[]{:S(2)}) %copy-start.8) | copy-done | bytes 16408
  24.0 0.0 copy-start.2
  24.0 0.0 copy-start.4
  24.0 0.0 copy-start.6
  24.0 0.0 copy-start.9
  24.0 4.6 %shard_map.87 = f32[16,104,128]{2,1,0:T(8,128)S(1)} custom-call(s32[1]{0:T(128)S(6)} %copy.9.flag_ref.refs_0_, f32[1024,512]{1,0:T(8,128)S(1)} %bitcast.10, bf16[1024,512]{1,0:T(8,128)(2,1)S(1)} %bitcast.8, s32[32,128]{1,0:T(8,128)S(1)} %reshape_squeeze.3.freq_ref, f32[16,8,128]{2,1,0:T(8,128)S(1)} %all-to-all-done.square_ref, bf16[128,64]{1,0:T(8,128)(2,1)S(1)} %copy-done.8), custom_call_target="tpu_custom_call" | custom-call | tf_op jit(solution)/shard_map/pallas_call | solution.py:229
  28.6 0.0 copy-start.5
  28.6 0.9 %copy-done.5 = f32[16,104,128]{2,1,0:T(8,128)} copy-done((f32[16,104,128]{2,1,0:T(8,128)}, f32[16,104,128]{2,1,0:T(8,128)S(1)}, u32[]{:S(2)}) %copy-start.5) | copy-done | bytes 851992
  29.5 6.8 %all-to-all-start.1 = ((f32[16,104,128]{2,1,0:T(8,128)}), f32[16,104,128]{2,1,0:T(8,128)}, u32[]{:S(2)}, u32[]{:S(2)}) async-start(f32[16,104,128]{2,1,0:T(8,128)} %copy-done.5), calls=%async_computation.1 | async-start | bytes 1703936 | tf_op jit(solution)/shard_map/all_to_all | solution.py:238
  36.3 0.8 %slice_bitcast_fusion.refs_3_ = f32[104,128]{1,0:T(8,128)S(1)} fusion(f32[16,104,128]{2,1,0:T(8,128)} %copy-done.5), kind=kLoop, calls=%fused_computation | loop fusion | bytes 106496 | tf_op jit(solution)/shard_map/squeeze | solution.py:237
  37.1 12.5 %all-to-all-done.1.refs_4_ = f32[16,104,128]{2,1,0:T(8,128)} async-done(((f32[16,104,128]{2,1,0:T(8,128)}), f32[16,104,128]{2,1,0:T(8,128)}, u32[]{:S(2)}, u32[]{:S(2)}) %all-to-all-start.1) | async-done | bytes 852000 | tf_op jit(solution)/shard_map/all_to_all | solution.py:238
  49.6 0.0 copy-done.2
  49.7 0.0 copy-done.4
  49.7 0.0 copy-done.6
  49.7 0.0 copy-done.9
  49.7 0.0 copy-start.7
  49.7 0.9 %copy-done.7 = bf16[2,256,256]{2,1,0:T(8,128)(2,1)S(1)} copy-done((bf16[2,256,256]{2,1,0:T(8,128)(2,1)S(1)}, bf16[2,256,256]{2,1,0:T(8,128)(2,1)}, u32[]{:S(2)}) %copy-start.7) | copy-done | bytes 262168
  50.6 20.9 %shard_map.88 = (f32[1024,512]{1,0:T(8,128)}, f32[1024,512]{1,0:T(8,128)}) custom-call(s32[1]{0:T(128)S(6)} %copy.9.flag_ref.refs_0_, f32[1024,512]{1,0:T(8,128)S(1)} %bitcast.11, bf16[1024,512]{1,0:T(8,128)(2,1)S(1)} %bitcast.9, f32[104,128]{1,0:T(8,128)S(1)} %slice_bitcast_fusion.refs_3_, f32[16,104,128]{2,1,0:T(8,128)} %all-to-all-done.1.refs_4_, ...), custom_call_target="tpu_custom_call" | custom-call | tf_op jit(solution)/shard_map/pallas_call | solution.py:240
Async XLA Ops:
  0.6 1.2 %copy-start = (bf16[1,1024,512]{2,1,0:T(8,128)(2,1)S(1)}, bf16[1,1024,512]{2,1,0:T(8,128)(2,1)}, u32[]{:S(2)}) copy-start(bf16[1,1024,512]{2,1,0:T(8,128)(2,1)} %param.8) | copy-start | bytes 3145732
  2.6 17.8 %all-to-all-start = ((f32[16,8,128]{2,1,0:T(8,128)}), f32[16,8,128]{2,1,0:T(8,128)S(1)}, u32[]{:S(2)}, u32[]{:S(2)}) async-start(f32[16,8,128]{2,1,0:T(8,128)} %shard_map.86), calls=%async_computation | async-start | bytes 131072 | tf_op jit(solution)/shard_map/all_to_all | solution.py:227
  20.4 1.2 %copy-start.1 = (bf16[1,1024,512]{2,1,0:T(8,128)(2,1)S(1)}, bf16[1,1024,512]{2,1,0:T(8,128)(2,1)}, u32[]{:S(2)}) copy-start(bf16[1,1024,512]{2,1,0:T(8,128)(2,1)} %param.8) | copy-start | bytes 3145732
  21.7 1.6 %copy-start.3 = (f32[1,1024,512]{2,1,0:T(8,128)S(1)}, f32[1,1024,512]{2,1,0:T(8,128)}, u32[]{:S(2)}) copy-start(f32[1,1024,512]{2,1,0:T(8,128)} %param.7) | copy-start | bytes 6291460
  23.2 0.8 %copy-start.8 = (bf16[128,64]{1,0:T(8,128)(2,1)S(1)}, bf16[128,64]{1,0:T(8,128)(2,1)}, u32[]{:S(2)}) copy-start(bf16[128,64]{1,0:T(8,128)(2,1)} %constant.6.clone.stacked_ref.refs_5_) | copy-start | bytes 49156
  24.0 25.6 %copy-start.2 = (bf16[1,1024,512]{2,1,0:T(8,128)(2,1)S(1)}, bf16[1,1024,512]{2,1,0:T(8,128)(2,1)}, u32[]{:S(2)}) copy-start(bf16[1,1024,512]{2,1,0:T(8,128)(2,1)} %param.8) | copy-start | bytes 3145732
  24.0 25.6 %copy-start.4 = (f32[1,1024,512]{2,1,0:T(8,128)S(1)}, f32[1,1024,512]{2,1,0:T(8,128)}, u32[]{:S(2)}) copy-start(f32[1,1024,512]{2,1,0:T(8,128)} %param.7) | copy-start | bytes 6291460
  24.0 25.6 %copy-start.6 = (bf16[2,256,256]{2,1,0:T(8,128)(2,1)S(1)}, bf16[2,256,256]{2,1,0:T(8,128)(2,1)}, u32[]{:S(2)}) copy-start(bf16[2,256,256]{2,1,0:T(8,128)(2,1)} %constant.8.clone.refs_7_) | copy-start | bytes 786436
  24.0 25.7 %copy-start.9 = (bf16[128,64]{1,0:T(8,128)(2,1)S(1)}, bf16[128,64]{1,0:T(8,128)(2,1)}, u32[]{:S(2)}) copy-start(bf16[128,64]{1,0:T(8,128)(2,1)} %constant.6.clone.stacked_ref.refs_5_) | copy-start | bytes 49156
  28.6 0.9 %copy-start.5 = (f32[16,104,128]{2,1,0:T(8,128)}, f32[16,104,128]{2,1,0:T(8,128)S(1)}, u32[]{:S(2)}) copy-start(f32[16,104,128]{2,1,0:T(8,128)S(1)} %shard_map.87) | copy-start | bytes 2555908
  29.5 20.1 %all-to-all-start.1 = ((f32[16,104,128]{2,1,0:T(8,128)}), f32[16,104,128]{2,1,0:T(8,128)}, u32[]{:S(2)}, u32[]{:S(2)}) async-start(f32[16,104,128]{2,1,0:T(8,128)} %copy-done.5), calls=%async_computation.1 | async-start | bytes 1703936 | tf_op jit(solution)/shard_map/all_to_all | solution.py:238
  49.7 1.0 %copy-start.7 = (bf16[2,256,256]{2,1,0:T(8,128)(2,1)S(1)}, bf16[2,256,256]{2,1,0:T(8,128)(2,1)}, u32[]{:S(2)}) copy-start(bf16[2,256,256]{2,1,0:T(8,128)(2,1)} %constant.7.clone.refs_6_) | copy-start | bytes 786436

commit v2 on v0

v2 whole, which is shorter than its diff:
```python
import math

import jax
import jax.numpy as jnp
import ml_dtypes
import numpy as np
from jax import lax
from jax.experimental import pallas as pl
from jax.experimental.pallas import tpu as pltpu
from jax.sharding import PartitionSpec as P

GROUP = 64
TOPK = 32
LANES = 128
TILE = (512, 256)
CLIP_RMS = 0.5
DECAY = 0.9
F32 = jnp.float32
BF16 = jnp.bfloat16


def split_table(table):
    high = table.astype(ml_dtypes.bfloat16)
    low = (table - high.astype(np.float64)).astype(ml_dtypes.bfloat16)
    return high, low


def tables():
    freq = np.arange(GROUP)[:, None]
    place = np.arange(GROUP)[None, :]
    table = np.sqrt(np.where(freq == 0, 1.0, 2.0) / GROUP) * np.cos(math.pi * (2 * place + 1) * freq / (2 * GROUP))
    high, low = split_table(table)
    stacked = np.concatenate([high.T, low.T], axis=0)
    eye = np.eye(4)
    rows = np.stack(split_table(np.kron(eye, table.T)))
    cols = np.stack(split_table(np.kron(eye, table)))
    return stacked, rows, cols


def halves(x):
    high = x.astype(BF16)
    return high, (x - high.astype(F32)).astype(BF16)


def dot(a, b):
    return jnp.dot(a, b, preferred_element_type=F32)


def dot_nt(a, b):
    return lax.dot_general(a, b, (((1,), (1,)), ((), ())), preferred_element_type=F32)


def square_kernel(grad_hbm, out_ref, grad, sems):
    pieces = grad.shape[0]
    rows = grad.shape[1]
    copies = [
        pltpu.make_async_copy(grad_hbm.at[pl.ds(n * rows, rows)], grad.at[n], sems.at[n]) for n in range(pieces)
    ]
    for copy in copies:
        copy.start()
    part = jnp.zeros((8, LANES), F32)
    for n, copy in enumerate(copies):
        copy.wait()
        g = grad[n].astype(F32)
        g = g * g
        g = g.reshape(-1, 8, g.shape[1]).sum(axis=0)
        part += sum(g[:, n * LANES:(n + 1) * LANES] for n in range(g.shape[1] // LANES))
    for n in range(out_ref.shape[0]):
        out_ref[n] = part


def table_rows(freqs, stacked):
    places, wide = [], freqs.shape[0] * LANES
    for n in (0, 1):
        index = lax.shift_right_logical(freqs, 6) if n == 0 else lax.bitwise_and(freqs, GROUP - 1)
        places += [index[s:s + 1, :] for s in range(freqs.shape[0])]
    row = lax.broadcasted_iota(jnp.int32, (GROUP, 2 * wide), 0)
    hot = jnp.where(row == jnp.concatenate(places, axis=1), 1.0, 0.0).astype(BF16)
    return dot(stacked, hot).astype(BF16)


def parts(table, s):
    a = slice(s * LANES, (s + 1) * LANES)
    b = slice((s + 8) * LANES, (s + 9) * LANES)
    return table[:GROUP, a], table[GROUP:, a], table[:GROUP, b], table[GROUP:, b]


def diagonal(x):
    lane = lax.broadcasted_iota(jnp.int32, x.shape, 1)
    zero = jnp.zeros_like(x)
    return jnp.concatenate([jnp.where(lane // TOPK == m, x, zero) for m in range(4)], axis=0)


def tile_of(step):
    return pl.ds(pl.multiple_of(step % 2 * TILE[0], TILE[0]), TILE[0]), pl.ds(pl.multiple_of(step // 2 * TILE[1], TILE[1]), TILE[1])


def fetch(mom_hbm, grad_hbm, mom, grad, sems):
    return [
        (
            pltpu.make_async_copy(mom_hbm.at[tile_of(n)], mom.at[n], sems.at[0, n]),
            pltpu.make_async_copy(grad_hbm.at[tile_of(n)], grad.at[n], sems.at[1, n]),
        )
        for n in range(4)
    ]


def arrive(step, mom_hbm, grad_hbm, mom, grad, sems):
    pltpu.make_async_copy(mom_hbm.at[tile_of(step)], mom.at[step], sems.at[0, step]).wait()
    pltpu.make_async_copy(grad_hbm.at[tile_of(step)], grad.at[step], sems.at[1, step]).wait()


def kept_kernel(flag_ref, mom_hbm, grad_hbm, freq_hbm, stacked_hbm, out_ref, mom, grad, sems, freq_ref, stacked_ref, small_sems, freq_rows, table):
    first = [
        pltpu.make_async_copy(freq_hbm, freq_ref, small_sems.at[0]),
        pltpu.make_async_copy(stacked_hbm, stacked_ref, small_sems.at[1]),
    ]
    for copy in first:
        copy.start()
    for pair in fetch(mom_hbm, grad_hbm, mom, grad, sems):
        for copy in pair:
            copy.start()
    for copy in first:
        copy.wait()
    for col in range(2):
        freq_rows[16 * col:16 * col + 16, :] = jnp.concatenate([freq_ref[:, 4 * col + m, :] for m in range(4)], axis=1)

    flag = (flag_ref[0] == 1).astype(F32)
    stacked = stacked_ref[...]
    chunks = freq_rows.shape[0]
    table[0] = table_rows(freq_rows[:8, :], stacked)

    def one(step, carry):
        at = pl.multiple_of(step * 8, 8)
        later = jnp.minimum(step + 1, 3)
        arrive(step, mom_hbm, grad_hbm, mom, grad, sems)
        freqs = freq_rows[pl.ds(at, 8), :]
        us, vs = [], []
        for s in range(8):
            rows = slice(s * GROUP, (s + 1) * GROUP)
            ah, al, bh, bl = parts(table.at[step % 2], s)
            weights = jnp.concatenate([diagonal(bh), diagonal(bl)], axis=1)
            xh, xl = halves(mom[step, rows, :])
            y = dot(jnp.concatenate([xh, xl, grad[step, rows, :]], axis=0), weights)
            y = y[:, :LANES] + y[:, LANES:]
            a = ah.astype(F32) + al.astype(F32)
            km = jnp.sum((y[:GROUP] + y[GROUP:2 * GROUP]) * a, axis=0, keepdims=True)
            kg = jnp.sum(y[2 * GROUP:] * a, axis=0, keepdims=True)
            us.append(DECAY * km + (1.0 - flag) * kg)
            vs.append(flag * kg)
        table[(step + 1) % 2] = table_rows(freq_rows[pl.ds(pl.multiple_of(later * 8, 8), 8), :], stacked)
        out_ref[pl.ds(at, 8), :] = jnp.concatenate(us, axis=0)
        out_ref[pl.ds(chunks + at, 8), :] = jnp.concatenate(vs, axis=0)
        out_ref[pl.ds(2 * chunks + at, 8), :] = freqs.astype(F32)
        return carry

    lax.fori_loop(0, 4, one, 0)


def message_kernel(kept_ref, square_ref, out_hbm, message, sems):
    rows = kept_ref.shape[0]
    message[:rows, :] = kept_ref[...]
    message[rows:, :] = jnp.sum(square_ref[...], axis=0)
    copies = [pltpu.make_async_copy(message, out_hbm.at[n], sems.at[n]) for n in range(out_hbm.shape[0])]
    for copy in copies:
        copy.start()
    for copy in copies:
        copy.wait()


def own_kernel(flag_ref, mom_hbm, grad_hbm, kept_ref, stacked_ref, u_ref, v_ref, mom, grad, sems):
    step = pl.program_id(0)

    @pl.when(step == 0)
    def _():
        for pair in fetch(mom_hbm, grad_hbm, mom, grad, sems):
            for copy in pair:
                copy.start()

    arrive(step, mom_hbm, grad_hbm, mom, grad, sems)
    flag = (flag_ref[0] == 1).astype(F32)
    stacked = stacked_ref[...]
    chunks = kept_ref.shape[0] // 3
    at = pl.multiple_of(step * 8, 8)
    us = kept_ref[pl.ds(at, 8), :]
    vs = kept_ref[pl.ds(chunks + at, 8), :]
    table = table_rows(kept_ref[pl.ds(2 * chunks + at, 8), :].astype(jnp.int32), stacked)
    for s in range(8):
        rows = slice(s * GROUP, (s + 1) * GROUP)
        ah, al, bh, bl = parts(table, s)
        a = ah.astype(F32) + al.astype(F32)
        high, low = halves(jnp.concatenate([a * us[s:s + 1, :], a * vs[s:s + 1, :]], axis=0))
        left = jnp.concatenate([high, low], axis=0)
        right = jnp.concatenate([high, jnp.zeros_like(low)], axis=0)
        y = dot_nt(jnp.concatenate([left, right], axis=1), jnp.concatenate([diagonal(bh), diagonal(bl)], axis=1))
        g = grad[step, rows, :].astype(F32)
        u_ref[rows, :] = DECAY * mom[step, rows, :] + (1.0 - flag) * g - (y[:GROUP] + y[2 * GROUP:3 * GROUP])
        v_ref[rows, :] = flag * g - (y[GROUP:2 * GROUP] + y[3 * GROUP:])


def update_kernel(count, all_ref, u_ref, v_ref, rows_ref, cols_ref, mom_out, update_out, lists_a, lists_b, lists_h, lists_l, pooled,
                  factor_ref):
    step = pl.program_id(0)
    replicas = all_ref.shape[0]
    chunks = (all_ref.shape[1] - 8) // 3

    @pl.when(step == 0)
    def _():
        total = jnp.sum(all_ref[:, 3 * chunks:, :], axis=0)
        total = jnp.sum(total, axis=(0, 1), keepdims=True)
        rms = jnp.sqrt(total * (1.0 / count))
        factor_ref[...] = jnp.broadcast_to(jnp.minimum(jnp.float32(1.0), CLIP_RMS / (rms + 1e-06)), factor_ref.shape)

    factor = factor_ref[...]
    lane = lax.broadcasted_iota(jnp.int32, (8, LANES), 1) // TOPK

    def regroup(xs, m):
        moved = [x if r == m else pltpu.roll(x, (TOPK * (r - m)) % LANES, 1) for r, x in enumerate(xs)]
        out = moved[0]
        for r in range(1, 4):
            out = jnp.where(lane == r, moved[r], out)
        return out

    def prepare(tile, slot):
        at = pl.multiple_of(tile * 8, 8)
        for group in range(replicas // 4):
            ks, fs = [], []
            for r in range(4 * group, 4 * group + 4):
                u = all_ref[r, pl.ds(at, 8), :]
                v = all_ref[r, pl.ds(chunks + at, 8), :]
                ks.append((u + factor * v) * (1.0 / replicas))
                fs.append(all_ref[r, pl.ds(2 * chunks + at, 8), :])
            for m in range(4):
                k = regroup(ks, m)
                f = regroup(fs, m).astype(jnp.int32)
                high = k.astype(BF16).astype(F32)
                place = slice(group * LANES, (group + 1) * LANES)
                lists_a[slot, m, :, place] = lax.shift_right_logical(f, 6)
                lists_b[slot, m, :, place] = lax.bitwise_and(f, GROUP - 1)
                lists_h[slot, m, :, place] = high
                lists_l[slot, m, :, place] = k - high

    items = replicas * TOPK
    place = lax.broadcasted_iota(jnp.int32, (GROUP, items), 0)

    def scatter(s, m, slot):
        here = slice(s, s + 1)
        hit = place == lists_a[slot, m, here, :]
        high = jnp.where(hit, lists_h[slot, m, here, :], 0.0).astype(BF16)
        low = jnp.where(hit, lists_l[slot, m, here, :], 0.0).astype(BF16)
        hot = jnp.where(place == lists_b[slot, m, here, :], 1.0, 0.0).astype(BF16)
        out = dot_nt(jnp.concatenate([high, low], axis=0), hot)
        return out[:GROUP] + out[GROUP:]

    def scatter_rows(first, last, slot):
        for s in range(first, last):
            for pair in range(2):
                both = jnp.concatenate([scatter(s, 2 * pair, slot), scatter(s, 2 * pair + 1, slot)], axis=1)
                pooled[slot, s * GROUP:(s + 1) * GROUP, pair * LANES:(pair + 1) * LANES] = both

    def columns(slot):
        ph, plow = halves(pooled[slot])
        ch, cl = cols_ref[0], cols_ref[1]
        return dot(ph, ch) + dot(plow, ch) + dot(ph, cl)

    def finish(y):
        rh, rl = rows_ref[0], rows_ref[1]
        for half in range(2):
            part = slice(half * 256, (half + 1) * 256)
            yh, yl = halves(y[part, :])
            update_out[part, :] = dot(rh, yh) + dot(rh, yl) + dot(rl, yh)

    def new_momentum():
        mom_out[...] = u_ref[...] + factor[:1, :1] * v_ref[...]

    @pl.when(step == 0)
    def _():
        prepare(0, 0)
        scatter_rows(0, 8, 0)
        new_momentum()
        prepare(1, 1)

    @pl.when(jnp.logical_and(step > 0, step < 4))
    def _():
        slot = step % 2
        y = columns(1 - slot)
        scatter_rows(0, 4, slot)
        finish(y)
        scatter_rows(4, 8, slot)
        new_momentum()
        prepare(jnp.minimum(step + 1, 3), 1 - slot)

    @pl.when(step == 4)
    def _():
        finish(columns(1))


def full(shape):
    return pl.BlockSpec(shape, lambda i: (0,) * len(shape))


def body(momentum, gradient, kept_freq, clip_flag):
    replicas, tensors = lax.axis_size("replica"), lax.axis_size("tensor")
    mom, grad, freq = momentum[0], gradient[0], kept_freq[0]
    rows, cols = mom.shape
    steps = 4
    chunks = rows // GROUP * cols // GROUP * TOPK // LANES
    stacked, row_table, col_table = (jnp.asarray(t) for t in tables())
    tile = pl.BlockSpec(TILE, lambda i: (i % 2, i // 2))
    scalar = pl.BlockSpec(memory_space=pltpu.SMEM)
    hbm = pl.BlockSpec(memory_space=pltpu.HBM)
    limit = pltpu.CompilerParams(vmem_limit_bytes=60 * 1024 * 1024)
    small = pltpu.CompilerParams(vmem_limit_bytes=32 * 1024 * 1024)
    landing = [pltpu.VMEM((steps,) + TILE, F32), pltpu.VMEM((steps,) + TILE, BF16), pltpu.SemaphoreType.DMA((2, steps))]

    squares = pl.pallas_call(
        square_kernel,
        in_specs=[hbm],
        out_specs=pl.BlockSpec(memory_space=pltpu.VMEM),
        out_shape=jax.ShapeDtypeStruct((tensors, 8, LANES), F32),
        scratch_shapes=[pltpu.VMEM((4, rows // 4, cols), BF16), pltpu.SemaphoreType.DMA((4,))],
        compiler_params=limit,
    )(grad)
    squares = lax.all_to_all(squares, "tensor", 0, 0)

    kept = pl.pallas_call(
        kept_kernel,
        in_specs=[scalar, hbm, hbm, hbm, hbm],
        out_specs=pl.BlockSpec(memory_space=pltpu.VMEM),
        out_shape=jax.ShapeDtypeStruct((3 * chunks, LANES), F32),
        scratch_shapes=landing
        + [
            pltpu.VMEM(freq.shape, jnp.int32),
            pltpu.VMEM(stacked.shape, BF16),
            pltpu.SemaphoreType.DMA((2,)),
            pltpu.VMEM((chunks, LANES), jnp.int32),
            pltpu.VMEM((2, 2 * GROUP, 16 * LANES), BF16),
        ],
        compiler_params=limit,
        cost_estimate=pl.CostEstimate(flops=2 * 10 ** 9, bytes_accessed=3 * 2 ** 20, transcendentals=0),
    )(clip_flag, mom, grad, freq, stacked)

    message = pl.pallas_call(
        message_kernel,
        in_specs=[pl.BlockSpec(memory_space=pltpu.VMEM)] * 2,
        out_specs=hbm,
        out_shape=jax.ShapeDtypeStruct((replicas, 3 * chunks + 8, LANES), F32),
        scratch_shapes=[pltpu.VMEM((3 * chunks + 8, LANES), F32), pltpu.SemaphoreType.DMA((replicas,))],
        compiler_params=small,
    )(kept, squares)
    everyone = lax.all_to_all(message, "replica", 0, 0)

    own_u, own_v = pl.pallas_call(
        own_kernel,
        grid=(steps,),
        in_specs=[scalar, hbm, hbm, full(kept.shape), full(stacked.shape)],
        out_specs=[tile, tile],
        out_shape=[jax.ShapeDtypeStruct((rows, cols), F32)] * 2,
        scratch_shapes=landing,
        compiler_params=limit,
        cost_estimate=pl.CostEstimate(flops=2 * 10 ** 9, bytes_accessed=7 * 2 ** 20, transcendentals=0),
    )(clip_flag, mom, grad, kept, stacked)

    early = pl.BlockSpec(TILE, lambda i: (jnp.minimum(i, 3) % 2, jnp.minimum(i, 3) // 2))
    late = pl.BlockSpec(TILE, lambda i: (jnp.maximum(i - 1, 0) % 2, jnp.maximum(i - 1, 0) // 2))
    new_mom, update = pl.pallas_call(
        lambda *refs: update_kernel(replicas * tensors * rows * cols, *refs),
        grid=(steps + 1,),
        in_specs=[full(everyone.shape), early, early, full(row_table.shape), full(col_table.shape)],
        out_specs=[early, late],
        out_shape=[jax.ShapeDtypeStruct((rows, cols), F32)] * 2,
        scratch_shapes=[pltpu.VMEM((2, 4, 8, replicas * TOPK), t) for t in (jnp.int32, jnp.int32, F32, F32)]
        + [pltpu.VMEM((2,) + TILE, F32), pltpu.VMEM((8, LANES), F32)],
        compiler_params=pltpu.CompilerParams(vmem_limit_bytes=58 * 1024 * 1024),
    )(everyone, own_u, own_v, row_table, col_table)
    return (new_mom[None], update)


def solution(mesh):
    placed = (
        P("replica", None, "tensor"),
        P("replica", None, "tensor"),
        P("replica", None, "tensor", None),
        P("replica"),
    )
    return jax.shard_map(
        body,
        mesh=mesh,
        in_specs=placed,
        out_specs=(P("replica", None, "tensor"), P(None, "tensor")),
        check_vma=False,
    )
```

time: 298 us -> 55.1 us (0.18)
  blocking collectives: 81.4 us -> 0 us
  local copies, waits for them, and re-layouts: 65.7 us -> 1.7 us
  waiting for transfers between devices: 69.4 us -> 9.43 us
  other arithmetic: 34.6 us -> 0 us
  matrix products: 30.7 us -> 0 us
  Pallas kernels: 0 us -> 24.9 us
  starting transfers between devices: 0.04 us -> 16.8 us
  between operations: 15.6 us -> 1.32 us
    psum x1 -> x0, blocking collectives: 81.4 us -> none  [body(): total = lax.psum(jnp.sum(grad * grad), ('replica', 'tensor'))]
    psum x1 -> x0, waiting for transfers between devices: 69.4 us -> none  [body(): pooled = lax.psum(sparse, 'replica')]
    gather x2 -> x0, local copies, waits for them, and re-layouts: 32 us -> none  [body(): kept = jnp.take_along_axis(flat, own_freq, axis=2)]
    dot_general x6 -> x0, matrix products: 30.7 us -> none  [the longest x2 11.7 us: inverse(): jnp.einsum('ap,ijab->ipjb', table, coef, precision=lax.Precision.HIGHEST)]
    pallas_call x0 -> x5, Pallas kernels: none -> 24.9 us  [the longest x1 11 us: body(): pl.pallas_call(lambda *refs: update_kernel(replicas * tensors * rows * co...]
    unnamed x4 -> x0, other arithmetic: 24.1 us -> none
    reshape x5 -> x0, local copies, waits for them, and re-layouts: 18.8 us -> none  [the longest x2 9.74 us: inverse(): return full.reshape(coef.shape[0] * width, coef.shape[1] * width)]
    all_to_all x0 -> x2, starting transfers between devices: none -> 16.8 us  [the longest x1 9.99 us: body(): squares = lax.all_to_all(squares, 'tensor', 0, 0)]
  transfers between devices with their start and end apart: 1 -> 2, of which waited for: 1 -> 2; matrix products, arithmetic and copies ran while one was open for 8% -> 0% of each run, Pallas kernels for 0% -> 20%
where the time goes in v2:
time: 55.1 us; the launch traced here: 54.2 us
  Pallas kernels  24.9 us (45%)
  starting transfers between devices  16.8 us (30%)
  waiting for transfers between devices  9.43 us (17%)
  local copies, waits for them, and re-layouts  1.7 us (3%)
  between operations  1.32 us (2%)
    pallas_call x1, Pallas kernels, body(): pl.pallas_call(lambda *refs: update_kernel(replicas * tensors * rows * co...  11 us
    all_to_all x1, starting transfers between devices, body(): squares = lax.all_to_all(squares, 'tensor', 0, 0)  9.99 us
    all_to_all x1, waiting for transfers between devices, body(): everyone = lax.all_to_all(message, 'replica', 0, 0)  7.01 us
    all_to_all x1, starting transfers between devices, body(): everyone = lax.all_to_all(message, 'replica', 0, 0)  6.77 us
    pallas_call x1, Pallas kernels, body(): pl.pallas_call(own_kernel, grid=(steps,), in_specs=[scalar, hbm, hbm, ful...  6.26 us
    pallas_call x1, Pallas kernels, body(): pl.pallas_call(kept_kernel, in_specs=[scalar, hbm, hbm, hbm, hbm], out_sp...  4.73 us
    all_to_all x1, waiting for transfers between devices, body(): squares = lax.all_to_all(squares, 'tensor', 0, 0)  2.42 us
    pallas_call x1, Pallas kernels, body(): pl.pallas_call(square_kernel, in_specs=[hbm], out_specs=pl.BlockSpec(memo...  1.88 us
  transfers between devices with their start and end apart: 2, of which 2 were waited for; matrix products, arithmetic and copies ran while one was open for 0% of the time, Pallas kernels for 20%

profile of v2, /device:TPU:1, one launch (start us, length us, event | category | flops | bytes accessed | tf_op | source)
XLA Modules:
  0.0 54.2 jit_solution(8214377034298188811)
XLA Ops:
  0.6 1.9 %shard_map.87 = f32[16,8,128]{2,1,0:T(8,128)} custom-call(bf16[1024,512]{1,0:T(8,128)(2,1)} %bitcast.4), custom_call_target="tpu_custom_call" | custom-call | tf_op jit(solution)/shard_map/pallas_call | solution.py:316
  2.5 10.0 %all-to-all-start = ((f32[16,8,128]{2,1,0:T(8,128)}), f32[16,8,128]{2,1,0:T(8,128)S(1)}, u32[]{:S(2)}, u32[]{:S(2)}) async-start(f32[16,8,128]{2,1,0:T(8,128)} %shard_map.87), calls=%async_computation | async-start | bytes 131072 | tf_op jit(solution)/shard_map/all_to_all | solution.py:324
  13.2 4.7 %shard_map.86.kept_ref = f32[96,128]{1,0:T(8,128)} custom-call(s32[1]{0:T(128)S(6)} %copy.9.flag_ref, f32[1024,512]{1,0:T(8,128)} %bitcast.7, bf16[1024,512]{1,0:T(8,128)(2,1)} %bitcast.5, s32[16,8,32]{2,1,0:T(8,128)} %bitcast.10, bf16[128,64]{1,0:T(8,128)(2,1)} %constant.6.clone.stacked_hbm.stacked_ref), custom_call_target="tpu_custom_call" | custom-call | flops 2000000000 | bytes 3145728 | tf_op jit(solution)/shard_map/pallas_call | solution.py:326
  17.9 2.4 %all-to-all-done.square_ref = f32[16,8,128]{2,1,0:T(8,128)S(1)} async-done(((f32[16,8,128]{2,1,0:T(8,128)}), f32[16,8,128]{2,1,0:T(8,128)S(1)}, u32[]{:S(2)}, u32[]{:S(2)}) %all-to-all-start) | async-done | bytes 65568 | tf_op jit(solution)/shard_map/all_to_all | solution.py:324
  20.3 0.0 copy-start
  20.3 0.8 %copy-done = f32[96,128]{1,0:T(8,128)S(1)} copy-done((f32[96,128]{1,0:T(8,128)S(1)}, f32[96,128]{1,0:T(8,128)}, u32[]{:S(2)}) %copy-start) | copy-done | bytes 49176
  21.1 1.0 %shard_map.88 = f32[16,104,128]{2,1,0:T(8,128)} custom-call(f32[96,128]{1,0:T(8,128)S(1)} %copy-done, f32[16,8,128]{2,1,0:T(8,128)S(1)} %all-to-all-done.square_ref), custom_call_target="tpu_custom_call" | custom-call | tf_op jit(solution)/shard_map/pallas_call | solution.py:343
  22.2 6.8 %all-to-all-start.1 = ((f32[16,104,128]{2,1,0:T(8,128)}), f32[16,104,128]{2,1,0:T(8,128)S(1)}, u32[]{:S(2)}, u32[]{:S(2)}) async-start(f32[16,104,128]{2,1,0:T(8,128)} %shard_map.88), calls=%async_computation.1 | async-start | bytes 1703936 | tf_op jit(solution)/shard_map/all_to_all | solution.py:351
  28.9 6.3 %shard_map.89 = (f32[1024,512]{1,0:T(8,128)}, f32[1024,512]{1,0:T(8,128)}) custom-call(s32[1]{0:T(128)S(6)} %copy.9.flag_ref, f32[1024,512]{1,0:T(8,128)} %bitcast.8, bf16[1024,512]{1,0:T(8,128)(2,1)} %bitcast.6, f32[96,128]{1,0:T(8,128)} %shard_map.86.kept_ref, bf16[128,64]{1,0:T(8,128)(2,1)} %constant.6.clone.stacked_hbm.stacked_ref), custom_call_target="tpu_custom_call" | custom-call | flops 2000000000 | bytes 7340032 | tf_op jit(solution)/shard_map/pallas_call | solution.py:353
  35.2 7.0 %all-to-all-done.1.refs_0_ = f32[16,104,128]{2,1,0:T(8,128)S(1)} async-done(((f32[16,104,128]{2,1,0:T(8,128)}), f32[16,104,128]{2,1,0:T(8,128)S(1)}, u32[]{:S(2)}, u32[]{:S(2)}) %all-to-all-start.1) | async-done | bytes 852000 | tf_op jit(solution)/shard_map/all_to_all | solution.py:351
  42.2 0.0 copy-start.1
  42.2 0.9 %copy-done.1 = f32[16,104,128]{2,1,0:T(8,128)} copy-done((f32[16,104,128]{2,1,0:T(8,128)}, f32[16,104,128]{2,1,0:T(8,128)S(1)}, u32[]{:S(2)}) %copy-start.1) | copy-done | bytes 851992
  43.1 11.0 %shard_map.90 = (f32[1024,512]{1,0:T(8,128)}, f32[1024,512]{1,0:T(8,128)}) custom-call(f32[16,104,128]{2,1,0:T(8,128)} %copy-done.1, f32[1024,512]{1,0:T(8,128)} %get-tuple-element.6.refs_1_, f32[1024,512]{1,0:T(8,128)} %get-tuple-element.7.refs_2_, bf16[2,256,256]{2,1,0:T(8,128)(2,1)} %constant.7.clone.refs_3_, bf16[2,256,256]{2,1,0:T(8,128)(2,1)} %constant.8.clone.refs_4_), custom_call_target="tpu_custom_call" | custom-call | tf_op jit(solution)/shard_map/pallas_call | solution.py:366
Async XLA Ops:
  2.5 17.8 %all-to-all-start = ((f32[16,8,128]{2,1,0:T(8,128)}), f32[16,8,128]{2,1,0:T(8,128)S(1)}, u32[]{:S(2)}, u32[]{:S(2)}) async-start(f32[16,8,128]{2,1,0:T(8,128)} %shard_map.87), calls=%async_computation | async-start | bytes 131072 | tf_op jit(solution)/shard_map/all_to_all | solution.py:324
  20.3 0.8 %copy-start = (f32[96,128]{1,0:T(8,128)S(1)}, f32[96,128]{1,0:T(8,128)}, u32[]{:S(2)}) copy-start(f32[96,128]{1,0:T(8,128)} %shard_map.86.kept_ref) | copy-start | bytes 147460
  22.2 20.1 %all-to-all-start.1 = ((f32[16,104,128]{2,1,0:T(8,128)}), f32[16,104,128]{2,1,0:T(8,128)S(1)}, u32[]{:S(2)}, u32[]{:S(2)}) async-start(f32[16,104,128]{2,1,0:T(8,128)} %shard_map.88), calls=%async_computation.1 | async-start | bytes 1703936 | tf_op jit(solution)/shard_map/all_to_all | solution.py:351
  42.2 0.9 %copy-start.1 = (f32[16,104,128]{2,1,0:T(8,128)}, f32[16,104,128]{2,1,0:T(8,128)S(1)}, u32[]{:S(2)}) copy-start(f32[16,104,128]{2,1,0:T(8,128)S(1)} %all-to-all-done.1.refs_0_) | copy-start | bytes 2555908

commit v3 on v2

v3 whole, which is shorter than its diff:
```python
import math

import jax
import jax.numpy as jnp
import ml_dtypes
import numpy as np
from jax import lax
from jax.experimental import pallas as pl
from jax.experimental.pallas import tpu as pltpu
from jax.sharding import PartitionSpec as P

GROUP = 64
TOPK = 32
LANES = 128
TILE = (512, 256)
CLIP_RMS = 0.5
DECAY = 0.9
F32 = jnp.float32
BF16 = jnp.bfloat16


def split_table(table):
    high = table.astype(ml_dtypes.bfloat16)
    low = (table - high.astype(np.float64)).astype(ml_dtypes.bfloat16)
    return high, low


def tables():
    freq = np.arange(GROUP)[:, None]
    place = np.arange(GROUP)[None, :]
    table = np.sqrt(np.where(freq == 0, 1.0, 2.0) / GROUP) * np.cos(math.pi * (2 * place + 1) * freq / (2 * GROUP))
    high, low = split_table(table)
    stacked = np.concatenate([high.T, low.T], axis=0)
    eye = np.eye(4)
    rows = np.stack(split_table(np.kron(eye, table.T)))
    cols = np.stack(split_table(np.kron(eye, table)))
    return stacked, rows, cols


def halves(x):
    high = x.astype(BF16)
    return high, (x - high.astype(F32)).astype(BF16)


def dot(a, b):
    return jnp.dot(a, b, preferred_element_type=F32)


def dot_nt(a, b):
    return lax.dot_general(a, b, (((1,), (1,)), ((), ())), preferred_element_type=F32)


def square_kernel(grad_hbm, mom_hbm, freq_hbm, square_hbm, grad_ref, mom_ref, freq_rows, freq_ref, squares, sems, grad_sems):
    pieces = 4
    rows = grad_ref.shape[0] // pieces
    small = pltpu.make_async_copy(freq_hbm, freq_ref, sems.at[0])
    large = []
    for n in range(pieces):
        here = pl.ds(n * rows, rows)
        large.append(pltpu.make_async_copy(grad_hbm.at[here], grad_ref.at[here], grad_sems.at[n]))
    rest = pltpu.make_async_copy(mom_hbm, mom_ref, sems.at[1])
    for copy in large + [small, rest]:
        copy.start()
    part = jnp.zeros((8, LANES), F32)
    for n, copy in enumerate(large):
        copy.wait()
        g = grad_ref[n * rows:(n + 1) * rows, :].astype(F32)
        g = g * g
        g = g.reshape(-1, 8, g.shape[1]).sum(axis=0)
        part += sum(g[:, m * LANES:(m + 1) * LANES] for m in range(g.shape[1] // LANES))
    for n in range(squares.shape[0]):
        squares[n] = part
    result = pltpu.make_async_copy(squares, square_hbm, sems.at[2])
    result.start()
    small.wait()
    for col in range(2):
        freq_rows[16 * col:16 * col + 16, :] = jnp.concatenate([freq_ref[:, 4 * col + m, :] for m in range(4)], axis=1)
    rest.wait()
    result.wait()


def table_rows(freqs, stacked):
    places, wide = [], freqs.shape[0] * LANES
    for n in (0, 1):
        index = lax.shift_right_logical(freqs, 6) if n == 0 else lax.bitwise_and(freqs, GROUP - 1)
        places += [index[s:s + 1, :] for s in range(freqs.shape[0])]
    row = lax.broadcasted_iota(jnp.int32, (GROUP, 2 * wide), 0)
    hot = jnp.where(row == jnp.concatenate(places, axis=1), 1.0, 0.0).astype(BF16)
    return dot(stacked, hot).astype(BF16)


def parts(table, s):
    a = slice(s * LANES, (s + 1) * LANES)
    b = slice((s + 8) * LANES, (s + 9) * LANES)
    return table[:GROUP, a], table[GROUP:, a], table[:GROUP, b], table[GROUP:, b]


def diagonal(x):
    lane = lax.broadcasted_iota(jnp.int32, x.shape, 1)
    zero = jnp.zeros_like(x)
    return jnp.concatenate([jnp.where(lane // TOPK == m, x, zero) for m in range(4)], axis=0)


def tile_of(step):
    return pl.multiple_of(step % 2 * TILE[0], TILE[0]), pl.ds(pl.multiple_of(step // 2 * TILE[1], TILE[1]), TILE[1])


def kept_kernel(flag_ref, mom_ref, grad_ref, freq_rows, stacked_ref, out_ref, table):
    flag = (flag_ref[0] == 1).astype(F32)
    stacked = stacked_ref[...]
    chunks = freq_rows.shape[0]
    table[0] = table_rows(freq_rows[:8, :], stacked)

    def one(step, carry):
        at = pl.multiple_of(step * 8, 8)
        later = pl.multiple_of(jnp.minimum(step + 1, 3) * 8, 8)
        top, cols = tile_of(step)
        freqs = freq_rows[pl.ds(at, 8), :]
        us, vs = [], []
        for s in range(8):
            rows = pl.ds(top + s * GROUP, GROUP)
            ah, al, bh, bl = parts(table.at[step % 2], s)
            weights = jnp.concatenate([diagonal(bh), diagonal(bl)], axis=1)
            xh, xl = halves(mom_ref[rows, cols])
            y = dot(jnp.concatenate([xh, xl, grad_ref[rows, cols]], axis=0), weights)
            y = y[:, :LANES] + y[:, LANES:]
            a = ah.astype(F32) + al.astype(F32)
            km = jnp.sum((y[:GROUP] + y[GROUP:2 * GROUP]) * a, axis=0, keepdims=True)
            kg = jnp.sum(y[2 * GROUP:] * a, axis=0, keepdims=True)
            us.append(DECAY * km + (1.0 - flag) * kg)
            vs.append(flag * kg)
        table[(step + 1) % 2] = table_rows(freq_rows[pl.ds(later, 8), :], stacked)
        out_ref[pl.ds(at, 8), :] = jnp.concatenate(us, axis=0)
        out_ref[pl.ds(chunks + at, 8), :] = jnp.concatenate(vs, axis=0)
        out_ref[pl.ds(2 * chunks + at, 8), :] = freqs.astype(F32)
        return carry

    lax.fori_loop(0, 4, one, 0)


def message_kernel(kept_ref, square_ref, out_hbm, message, sems):
    rows = kept_ref.shape[0]
    message[:rows, :] = kept_ref[...]
    message[rows:, :] = jnp.sum(square_ref[...], axis=0)
    copies = [pltpu.make_async_copy(message, out_hbm.at[n], sems.at[n]) for n in range(out_hbm.shape[0])]
    for copy in copies:
        copy.start()
    for copy in copies:
        copy.wait()


def tile_copies(step, pairs, sems):
    top, cols = tile_of(step)
    out = []
    for n, (hbm, tiles, outward) in enumerate(pairs):
        far, near = hbm.at[pl.ds(top, TILE[0]), cols], tiles.at[step]
        out.append(pltpu.make_async_copy(near if outward else far, far if outward else near, sems.at[n, step]))
    return out


def own_kernel(flag_ref, mom_hbm, grad_hbm, kept_ref, stacked_ref, u_hbm, v_hbm, mom, grad, u_out, v_out, in_sems, out_sems):
    inward = [(mom_hbm, mom, False), (grad_hbm, grad, False)]
    outward = [(u_hbm, u_out, True), (v_hbm, v_out, True)]
    for step in range(4):
        for copy in tile_copies(step, inward, in_sems):
            copy.start()
    flag = (flag_ref[0] == 1).astype(F32)
    stacked = stacked_ref[...]
    chunks = kept_ref.shape[0] // 3

    def one(step, carry):
        at = pl.multiple_of(step * 8, 8)
        us = kept_ref[pl.ds(at, 8), :]
        vs = kept_ref[pl.ds(chunks + at, 8), :]
        table = table_rows(kept_ref[pl.ds(2 * chunks + at, 8), :].astype(jnp.int32), stacked)
        for copy in tile_copies(step, inward, in_sems):
            copy.wait()
        for s in range(8):
            rows = slice(s * GROUP, (s + 1) * GROUP)
            ah, al, bh, bl = parts(table, s)
            a = ah.astype(F32) + al.astype(F32)
            high, low = halves(jnp.concatenate([a * us[s:s + 1, :], a * vs[s:s + 1, :]], axis=0))
            left = jnp.concatenate([high, low], axis=0)
            right = jnp.concatenate([high, jnp.zeros_like(low)], axis=0)
            y = dot_nt(jnp.concatenate([left, right], axis=1), jnp.concatenate([diagonal(bh), diagonal(bl)], axis=1))
            g = grad[step, rows, :].astype(F32)
            u_out[step, rows, :] = DECAY * mom[step, rows, :] + (1.0 - flag) * g - (y[:GROUP] + y[2 * GROUP:3 * GROUP])
            v_out[step, rows, :] = flag * g - (y[GROUP:2 * GROUP] + y[3 * GROUP:])
        for copy in tile_copies(step, outward, out_sems):
            copy.start()
        return carry

    lax.fori_loop(0, 4, one, 0)
    for step in range(4):
        for copy in tile_copies(step, outward, out_sems):
            copy.wait()


def update_kernel(count, all_ref, u_hbm, v_hbm, rows_ref, cols_ref, mom_hbm, update_hbm, lists_a, lists_b, lists_h, lists_l, pooled,
                  u_ref, v_ref, mom_out, update_out, in_sems, mom_sems, update_sems):
    inward = [(u_hbm, u_ref, False), (v_hbm, v_ref, False)]
    for tile in range(4):
        for copy in tile_copies(tile, inward, in_sems):
            copy.start()
    replicas = all_ref.shape[0]
    chunks = (all_ref.shape[1] - 8) // 3
    total = jnp.sum(all_ref[:, 3 * chunks:, :], axis=0)
    total = jnp.sum(total, axis=(0, 1), keepdims=True)
    rms = jnp.sqrt(total * (1.0 / count))
    factor = jnp.minimum(jnp.float32(1.0), CLIP_RMS / (rms + 1e-06))
    lane = lax.broadcasted_iota(jnp.int32, (8, LANES), 1) // TOPK
    half = TILE[0] // 2

    def regroup(xs, m):
        moved = [x if r == m else pltpu.roll(x, (TOPK * (r - m)) % LANES, 1) for r, x in enumerate(xs)]
        out = moved[0]
        for r in range(1, 4):
            out = jnp.where(lane == r, moved[r], out)
        return out

    def prepare(tile, slot):
        at = pl.multiple_of(tile * 8, 8)
        for group in range(replicas // 4):
            ks, fs = [], []
            for r in range(4 * group, 4 * group + 4):
                u = all_ref[r, pl.ds(at, 8), :]
                v = all_ref[r, pl.ds(chunks + at, 8), :]
                ks.append((u + factor * v) * (1.0 / replicas))
                fs.append(all_ref[r, pl.ds(2 * chunks + at, 8), :])
            for m in range(4):
                k = regroup(ks, m)
                f = regroup(fs, m).astype(jnp.int32)
                high = k.astype(BF16).astype(F32)
                place = slice(group * LANES, (group + 1) * LANES)
                lists_a[slot, m, :, place] = lax.shift_right_logical(f, 6)
                lists_b[slot, m, :, place] = lax.bitwise_and(f, GROUP - 1)
                lists_h[slot, m, :, place] = high
                lists_l[slot, m, :, place] = k - high

    items = replicas * TOPK
    place = lax.broadcasted_iota(jnp.int32, (GROUP, items), 0)

    def scatter(s, m, slot):
        here = slice(s, s + 1)
        hit = place == lists_a[slot, m, here, :]
        high = jnp.where(hit, lists_h[slot, m, here, :], 0.0).astype(BF16)
        low = jnp.where(hit, lists_l[slot, m, here, :], 0.0).astype(BF16)
        hot = jnp.where(place == lists_b[slot, m, here, :], 1.0, 0.0).astype(BF16)
        out = dot_nt(jnp.concatenate([high, low], axis=0), hot)
        return out[:GROUP] + out[GROUP:]

    def scatter_rows(part, slot):
        for s in range(4):
            for pair in range(2):
                both = [scatter(4 * part + s, 2 * pair + n, slot) for n in range(2)]
                pooled[part, s * GROUP:(s + 1) * GROUP, pair * LANES:(pair + 1) * LANES] = jnp.concatenate(both, axis=1)

    def inverse(tile, part):
        ph, plow = halves(pooled[part])
        ch, cl = cols_ref[0], cols_ref[1]
        yh, yl = halves(dot(ph, ch) + dot(plow, ch) + dot(ph, cl))
        rh, rl = rows_ref[0], rows_ref[1]
        update_out[tile, part] = dot(rh, yh) + dot(rh, yl) + dot(rl, yh)

    def update_copy(tile, part):
        top, cols = tile_of(tile)
        there = update_hbm.at[pl.ds(top + part * half, half), cols]
        return pltpu.make_async_copy(update_out.at[tile, part], there, update_sems.at[tile, part])

    def mom_copy(tile):
        return tile_copies(tile, [(mom_hbm, mom_out, True)], mom_sems)[0]

    pooled[1] = jnp.zeros(pooled.shape[1:], F32)
    prepare(0, 0)

    def one(tile, carry):
        slot = tile % 2
        before = jnp.maximum(tile - 1, 0)
        scatter_rows(0, slot)
        inverse(before, 1)
        scatter_rows(1, slot)
        inverse(tile, 0)
        for copy in tile_copies(tile, inward, in_sems):
            copy.wait()
        mom_out[tile] = u_ref[tile] + factor * v_ref[tile]
        prepare(jnp.minimum(tile + 1, 3), 1 - slot)
        mom_copy(tile).start()
        update_copy(tile, 0).start()

        @pl.when(tile > 0)
        def _():
            update_copy(before, 1).start()

        return carry

    lax.fori_loop(0, 4, one, 0)
    inverse(3, 1)
    update_copy(3, 1).start()
    for tile in range(4):
        mom_copy(tile).wait()
        for part in range(2):
            update_copy(tile, part).wait()


def body(momentum, gradient, kept_freq, clip_flag):
    replicas, tensors = lax.axis_size("replica"), lax.axis_size("tensor")
    mom, grad, freq = momentum[0], gradient[0], kept_freq[0]
    rows, cols = mom.shape
    chunks = rows // GROUP * cols // GROUP * TOPK // LANES
    stacked, row_table, col_table = (jnp.asarray(t) for t in tables())
    scalar = pl.BlockSpec(memory_space=pltpu.SMEM)
    hbm = pl.BlockSpec(memory_space=pltpu.HBM)
    vmem = pl.BlockSpec(memory_space=pltpu.VMEM)
    limit = pltpu.CompilerParams(vmem_limit_bytes=32 * 1024 * 1024)
    far = lambda x: pltpu.with_memory_space_constraint(x, pltpu.HBM)
    near = lambda x: pltpu.with_memory_space_constraint(x, pltpu.VMEM)

    squares, grad_near, mom_near, freq_rows = pl.pallas_call(
        square_kernel,
        in_specs=[hbm] * 3,
        out_specs=[hbm] + [vmem] * 3,
        out_shape=[
            pltpu.HBM((tensors, 8, LANES), F32),
            pltpu.VMEM(grad.shape, BF16),
            pltpu.VMEM(mom.shape, F32),
            pltpu.VMEM((chunks, LANES), jnp.int32),
        ],
        scratch_shapes=[
            pltpu.VMEM(freq.shape, jnp.int32),
            pltpu.VMEM((tensors, 8, LANES), F32),
            pltpu.SemaphoreType.DMA((3,)),
            pltpu.SemaphoreType.DMA((4,)),
        ],
        compiler_params=limit,
    )(far(grad), far(mom), far(freq))
    squares = lax.all_to_all(squares, "tensor", 0, 0)

    kept = pl.pallas_call(
        kept_kernel,
        in_specs=[scalar] + [vmem] * 4,
        out_specs=vmem,
        out_shape=pltpu.VMEM((3 * chunks, LANES), F32),
        scratch_shapes=[pltpu.VMEM((2, 2 * GROUP, 16 * LANES), BF16)],
        compiler_params=limit,
        cost_estimate=pl.CostEstimate(flops=2 * 10 ** 9, bytes_accessed=3 * 2 ** 20, transcendentals=0),
    )(clip_flag, near(mom_near), near(grad_near), near(freq_rows), near(stacked))

    message = pl.pallas_call(
        message_kernel,
        in_specs=[vmem] * 2,
        out_specs=hbm,
        out_shape=pltpu.HBM((replicas, 3 * chunks + 8, LANES), F32),
        scratch_shapes=[pltpu.VMEM((3 * chunks + 8, LANES), F32), pltpu.SemaphoreType.DMA((replicas,))],
        compiler_params=limit,
    )(near(kept), near(squares))
    everyone = lax.all_to_all(message, "replica", 0, 0)

    own_u, own_v = pl.pallas_call(
        own_kernel,
        in_specs=[scalar, hbm, hbm, vmem, vmem],
        out_specs=[hbm] * 2,
        out_shape=[pltpu.HBM((rows, cols), F32)] * 2,
        scratch_shapes=[pltpu.VMEM((4,) + TILE, t) for t in (F32, BF16, F32, F32)] + [pltpu.SemaphoreType.DMA((2, 4))] * 2,
        compiler_params=limit,
        cost_estimate=pl.CostEstimate(flops=2 * 10 ** 9, bytes_accessed=7 * 2 ** 20, transcendentals=0),
    )(clip_flag, far(mom), far(grad), near(kept), near(stacked))

    new_mom, update = pl.pallas_call(
        lambda *refs: update_kernel(replicas * tensors * rows * cols, *refs),
        in_specs=[vmem, hbm, hbm, vmem, vmem],
        out_specs=[hbm] * 2,
        out_shape=[jax.ShapeDtypeStruct((rows, cols), F32)] * 2,
        scratch_shapes=[pltpu.VMEM((2, 4, 8, replicas * TOPK), t) for t in (jnp.int32, jnp.int32, F32, F32)]
        + [
            pltpu.VMEM((2, TILE[0] // 2, TILE[1]), F32),
            pltpu.VMEM((4,) + TILE, F32),
            pltpu.VMEM((4,) + TILE, F32),
            pltpu.VMEM((4,) + TILE, F32),
            pltpu.VMEM((4, 2, TILE[0] // 2, TILE[1]), F32),
            pltpu.SemaphoreType.DMA((2, 4)),
            pltpu.SemaphoreType.DMA((1, 4)),
            pltpu.SemaphoreType.DMA((4, 2)),
        ],
        compiler_params=limit,
    )(near(everyone), far(own_u), far(own_v), near(row_table), near(col_table))
    return (new_mom[None], update)


def solution(mesh):
    placed = (
        P("replica", None, "tensor"),
        P("replica", None, "tensor"),
        P("replica", None, "tensor", None),
        P("replica"),
    )
    return jax.shard_map(
        body,
        mesh=mesh,
        in_specs=placed,
        out_specs=(P("replica", None, "tensor"), P(None, "tensor")),
        check_vma=False,
    )
```

time: 55.1 us -> 53.1 us (0.964)
  Pallas kernels: 24.9 us -> 21.3 us
  waiting for transfers between devices: 9.43 us -> 12.8 us
  local copies, waits for them, and re-layouts: 1.7 us -> 0.02 us
    pallas_call x4, Pallas kernels: 13.9 us -> 10.6 us  [the longest x1 5.15 us: body(): pl.pallas_call(own_kernel, in_specs=[scalar, hbm, hbm, vmem, vmem], out_s...]
    all_to_all x1, waiting for transfers between devices: 2.42 us -> 4.71 us  [body(): squares = lax.all_to_all(squares, 'tensor', 0, 0)]
    unnamed x4 -> x6, local copies, waits for them, and re-layouts: 1.7 us -> 0.02 us
    all_to_all x1, waiting for transfers between devices: 7.01 us -> 8.1 us  [body(): everyone = lax.all_to_all(message, 'replica', 0, 0)]
  transfers between devices with their start and end apart: 2 -> 2, of which waited for: 2 -> 2; matrix products, arithmetic and copies ran while one was open for 0% -> 0% of each run, Pallas kernels for 20% -> 14%
where the time goes in v3:
time: 53.1 us; the launch traced here: 52.3 us
  Pallas kernels  21.3 us (40%)
  starting transfers between devices  16.8 us (32%)
  waiting for transfers between devices  12.8 us (24%)
  between operations  1.35 us (3%)
    pallas_call x1, Pallas kernels, body(): pl.pallas_call(lambda *refs: update_kernel(replicas * tensors * rows * co...  10.7 us
    all_to_all x1, starting transfers between devices, body(): squares = lax.all_to_all(squares, 'tensor', 0, 0)  9.99 us
    all_to_all x1, waiting for transfers between devices, body(): everyone = lax.all_to_all(message, 'replica', 0, 0)  8.1 us
    all_to_all x1, starting transfers between devices, body(): everyone = lax.all_to_all(message, 'replica', 0, 0)  6.77 us
    pallas_call x1, Pallas kernels, body(): pl.pallas_call(own_kernel, in_specs=[scalar, hbm, hbm, vmem, vmem], out_s...  5.15 us
    all_to_all x1, waiting for transfers between devices, body(): squares = lax.all_to_all(squares, 'tensor', 0, 0)  4.71 us
    pallas_call x1, Pallas kernels, body(): pl.pallas_call(kept_kernel, in_specs=[scalar] + [vmem] * 4, out_specs=vme...  2.43 us
    pallas_call x1, Pallas kernels, body(): pl.pallas_call(square_kernel, in_specs=[hbm] * 3, out_specs=[hbm] + [vmem...  2.02 us
  transfers between devices with their start and end apart: 2, of which 2 were waited for; matrix products, arithmetic and copies ran while one was open for 0% of the time, Pallas kernels for 14%

profile of v3, /device:TPU:1, one launch (start us, length us, event | category | flops | bytes accessed | tf_op | source)
XLA Modules:
  0.0 52.3 jit_solution(8388097665816825732)
XLA Ops:
  0.6 0.0 copy-start.2
  0.6 2.0 %shard_map.86 = (f32[16,8,128]{2,1,0:T(8,128)}, bf16[1024,512]{1,0:T(8,128)(2,1)S(1)}, f32[1024,512]{1,0:T(8,128)S(1)}, s32[32,128]{1,0:T(8,128)S(1)}) custom-call(bf16[1024,512]{1,0:T(8,128)(2,1)} %bitcast.6, f32[1024,512]{1,0:T(8,128)} %bitcast.4, s32[16,8,32]{2,1,0:T(8,128)} %bitcast.8), custom_call_target="tpu_custom_call" | custom-call | tf_op jit(solution)/shard_map/pallas_call | solution.py:318
  2.7 10.0 %all-to-all-start = ((f32[16,8,128]{2,1,0:T(8,128)}), f32[16,8,128]{2,1,0:T(8,128)S(1)}, u32[]{:S(2)}, u32[]{:S(2)}) async-start(f32[16,8,128]{2,1,0:T(8,128)} %get-tuple-element.13), calls=%async_computation | async-start | bytes 131072 | tf_op jit(solution)/shard_map/all_to_all | solution.py:336
  13.3 0.0 copy-done.2
  13.3 2.4 %shard_map.87.kept_ref = f32[96,128]{1,0:T(8,128)S(1)} custom-call(s32[1]{0:T(128)S(6)} %copy.9.flag_ref, f32[1024,512]{1,0:T(8,128)S(1)} %get-tuple-element.10.mom_ref, bf16[1024,512]{1,0:T(8,128)(2,1)S(1)} %get-tuple-element.11.grad_ref, s32[32,128]{1,0:T(8,128)S(1)} %get-tuple-element.12.freq_rows, bf16[128,64]{1,0:T(8,128)(2,1)S(1)} %copy-done.2), custom_call_target="tpu_custom_call" | custom-call | flops 2000000000 | bytes 3145728 | tf_op jit(solution)/shard_map/pallas_call | solution.py:338
  15.8 4.7 %all-to-all-done.square_ref = f32[16,8,128]{2,1,0:T(8,128)S(1)} async-done(((f32[16,8,128]{2,1,0:T(8,128)}), f32[16,8,128]{2,1,0:T(8,128)S(1)}, u32[]{:S(2)}, u32[]{:S(2)}) %all-to-all-start) | async-done | bytes 65568 | tf_op jit(solution)/shard_map/all_to_all | solution.py:336
  20.5 1.0 %shard_map.88 = f32[16,104,128]{2,1,0:T(8,128)} custom-call(f32[96,128]{1,0:T(8,128)S(1)} %shard_map.87.kept_ref, f32[16,8,128]{2,1,0:T(8,128)S(1)} %all-to-all-done.square_ref), custom_call_target="tpu_custom_call" | custom-call | tf_op jit(solution)/shard_map/pallas_call | solution.py:348
  21.5 6.8 %all-to-all-start.1 = ((f32[16,104,128]{2,1,0:T(8,128)}), f32[16,104,128]{2,1,0:T(8,128)S(1)}, u32[]{:S(2)}, u32[]{:S(2)}) async-start(f32[16,104,128]{2,1,0:T(8,128)} %shard_map.88), calls=%async_computation.1 | async-start | bytes 1703936 | tf_op jit(solution)/shard_map/all_to_all | solution.py:356
  28.3 0.0 copy-start
  28.3 0.0 copy-start.1
  28.3 5.2 %shard_map.89 = (f32[1024,512]{1,0:T(8,128)}, f32[1024,512]{1,0:T(8,128)}) custom-call(s32[1]{0:T(128)S(6)} %copy.9.flag_ref, f32[1024,512]{1,0:T(8,128)} %bitcast.5, bf16[1024,512]{1,0:T(8,128)(2,1)} %bitcast.7, f32[96,128]{1,0:T(8,128)S(1)} %shard_map.87.kept_ref, bf16[128,64]{1,0:T(8,128)(2,1)S(1)} %copy-done.2), custom_call_target="tpu_custom_call" | custom-call | flops 2000000000 | bytes 7340032 | tf_op jit(solution)/shard_map/pallas_call | solution.py:358
  33.5 8.1 %all-to-all-done.1.refs_0_ = f32[16,104,128]{2,1,0:T(8,128)S(1)} async-done(((f32[16,104,128]{2,1,0:T(8,128)}), f32[16,104,128]{2,1,0:T(8,128)S(1)}, u32[]{:S(2)}, u32[]{:S(2)}) %all-to-all-start.1) | async-done | bytes 852000 | tf_op jit(solution)/shard_map/all_to_all | solution.py:356
  41.6 0.0 copy-done
  41.6 0.0 copy-done.1
  41.6 10.7 %shard_map.90 = (f32[1024,512]{1,0:T(8,128)}, f32[1024,512]{1,0:T(8,128)}) custom-call(f32[16,104,128]{2,1,0:T(8,128)S(1)} %all-to-all-done.1.refs_0_, f32[1024,512]{1,0:T(8,128)} %get-tuple-element.14.refs_1_, f32[1024,512]{1,0:T(8,128)} %get-tuple-element.15.refs_2_, bf16[2,256,256]{2,1,0:T(8,128)(2,1)S(1)} %copy-done.1, bf16[2,256,256]{2,1,0:T(8,128)(2,1)S(1)} %copy-done), custom_call_target="tpu_custom_call" | custom-call | tf_op jit(solution)/shard_map/pallas_call | solution.py:368
Async XLA Ops:
  0.6 12.7 %copy-start.2 = (bf16[128,64]{1,0:T(8,128)(2,1)S(1)}, bf16[128,64]{1,0:T(8,128)(2,1)}, u32[]{:S(2)}) copy-start(bf16[128,64]{1,0:T(8,128)(2,1)} %constant.6.clone.stacked_ref) | copy-start | bytes 49156
  2.7 17.8 %all-to-all-start = ((f32[16,8,128]{2,1,0:T(8,128)}), f32[16,8,128]{2,1,0:T(8,128)S(1)}, u32[]{:S(2)}, u32[]{:S(2)}) async-start(f32[16,8,128]{2,1,0:T(8,128)} %get-tuple-element.13), calls=%async_computation | async-start | bytes 131072 | tf_op jit(solution)/shard_map/all_to_all | solution.py:336
  21.5 20.1 %all-to-all-start.1 = ((f32[16,104,128]{2,1,0:T(8,128)}), f32[16,104,128]{2,1,0:T(8,128)S(1)}, u32[]{:S(2)}, u32[]{:S(2)}) async-start(f32[16,104,128]{2,1,0:T(8,128)} %shard_map.88), calls=%async_computation.1 | async-start | bytes 1703936 | tf_op jit(solution)/shard_map/all_to_all | solution.py:356
  28.3 13.3 %copy-start = (bf16[2,256,256]{2,1,0:T(8,128)(2,1)S(1)}, bf16[2,256,256]{2,1,0:T(8,128)(2,1)}, u32[]{:S(2)}) copy-start(bf16[2,256,256]{2,1,0:T(8,128)(2,1)} %constant.8.clone.refs_4_) | copy-start | bytes 786436
  28.3 13.3 %copy-start.1 = (bf16[2,256,256]{2,1,0:T(8,128)(2,1)S(1)}, bf16[2,256,256]{2,1,0:T(8,128)(2,1)}, u32[]{:S(2)}) copy-start(bf16[2,256,256]{2,1,0:T(8,128)(2,1)} %constant.7.clone.refs_3_) | copy-start | bytes 786436

commit v4 on v3

--- a/solution.py
+++ b/solution.py
@@ -31,9 +31,10 @@
     table = np.sqrt(np.where(freq == 0, 1.0, 2.0) / GROUP) * np.cos(math.pi * (2 * place + 1) * freq / (2 * GROUP))
     high, low = split_table(table)
     stacked = np.concatenate([high.T, low.T], axis=0)
-    eye = np.eye(4)
-    rows = np.stack(split_table(np.kron(eye, table.T)))
-    cols = np.stack(split_table(np.kron(eye, table)))
+    pair = [np.kron(np.eye(2), t.astype(np.float64)) for t in (high, low)]
+    none = np.zeros_like(pair[0])
+    cols = np.block([[pair[0], pair[1]], [pair[0], none]]).astype(ml_dtypes.bfloat16)
+    rows = np.block([[pair[0].T, pair[0].T], [pair[1].T, none]]).astype(ml_dtypes.bfloat16)
     return stacked, rows, cols
 
 
@@ -50,7 +51,7 @@
     return lax.dot_general(a, b, (((1,), (1,)), ((), ())), preferred_element_type=F32)
 
 
-def square_kernel(grad_hbm, mom_hbm, freq_hbm, square_hbm, grad_ref, mom_ref, freq_rows, freq_ref, squares, sems, grad_sems):
+def square_kernel(grad_hbm, freq_hbm, square_hbm, grad_ref, freq_rows, freq_ref, squares, sems, grad_sems):
     pieces = 4
     rows = grad_ref.shape[0] // pieces
     small = pltpu.make_async_copy(freq_hbm, freq_ref, sems.at[0])
@@ -58,8 +59,7 @@
     for n in range(pieces):
         here = pl.ds(n * rows, rows)
         large.append(pltpu.make_async_copy(grad_hbm.at[here], grad_ref.at[here], grad_sems.at[n]))
-    rest = pltpu.make_async_copy(mom_hbm, mom_ref, sems.at[1])
-    for copy in large + [small, rest]:
+    for copy in large + [small]:
         copy.start()
     part = jnp.zeros((8, LANES), F32)
     for n, copy in enumerate(large):
@@ -70,12 +70,11 @@
         part += sum(g[:, m * LANES:(m + 1) * LANES] for m in range(g.shape[1] // LANES))
     for n in range(squares.shape[0]):
         squares[n] = part
-    result = pltpu.make_async_copy(squares, square_hbm, sems.at[2])
+    result = pltpu.make_async_copy(squares, square_hbm, sems.at[1])
     result.start()
     small.wait()
     for col in range(2):
         freq_rows[16 * col:16 * col + 16, :] = jnp.concatenate([freq_ref[:, 4 * col + m, :] for m in range(4)], axis=1)
-    rest.wait()
     result.wait()
 
 
@@ -105,7 +104,20 @@
     return pl.multiple_of(step % 2 * TILE[0], TILE[0]), pl.ds(pl.multiple_of(step // 2 * TILE[1], TILE[1]), TILE[1])
 
 
-def kept_kernel(flag_ref, mom_ref, grad_ref, freq_rows, stacked_ref, out_ref, table):
+def tile_copies(step, pairs, sems):
+    top, cols = tile_of(step)
+    out = []
+    for n, (hbm, tiles, outward) in enumerate(pairs):
+        far, near = hbm.at[pl.ds(top, TILE[0]), cols], tiles.at[step]
+        out.append(pltpu.make_async_copy(near if outward else far, far if outward else near, sems.at[n, step]))
+    return out
+
+
+def kept_kernel(flag_ref, mom_hbm, grad_ref, freq_rows, stacked_ref, out_ref, message_hbm, mom, table, in_sems, out_sems):
+    inward = [(mom_hbm, mom, False)]
+    for step in range(4):
+        for copy in tile_copies(step, inward, in_sems):
+            copy.start()
     flag = (flag_ref[0] == 1).astype(F32)
     stacked = stacked_ref[...]
     chunks = freq_rows.shape[0]
@@ -116,13 +128,15 @@
         later = pl.multiple_of(jnp.minimum(step + 1, 3) * 8, 8)
         top, cols = tile_of(step)
         freqs = freq_rows[pl.ds(at, 8), :]
+        for copy in tile_copies(step, inward, in_sems):
+            copy.wait()
         us, vs = [], []
         for s in range(8):
-            rows = pl.ds(top + s * GROUP, GROUP)
+            rows = slice(s * GROUP, (s + 1) * GROUP)
             ah, al, bh, bl = parts(table.at[step % 2], s)
             weights = jnp.concatenate([diagonal(bh), diagonal(bl)], axis=1)
-            xh, xl = halves(mom_ref[rows, cols])
-            y = dot(jnp.concatenate([xh, xl, grad_ref[rows, cols]], axis=0), weights)
+            xh, xl = halves(mom[step, rows, :])
+            y = dot(jnp.concatenate([xh, xl, grad_ref[pl.ds(top + s * GROUP, GROUP), cols]], axis=0), weights)
             y = y[:, :LANES] + y[:, LANES:]
             a = ah.astype(F32) + al.astype(F32)
             km = jnp.sum((y[:GROUP] + y[GROUP:2 * GROUP]) * a, axis=0, keepdims=True)
@@ -136,26 +150,24 @@
         return carry
 
     lax.fori_loop(0, 4, one, 0)
-
-
-def message_kernel(kept_ref, square_ref, out_hbm, message, sems):
-    rows = kept_ref.shape[0]
-    message[:rows, :] = kept_ref[...]
-    message[rows:, :] = jnp.sum(square_ref[...], axis=0)
-    copies = [pltpu.make_async_copy(message, out_hbm.at[n], sems.at[n]) for n in range(out_hbm.shape[0])]
+    copies = [
+        pltpu.make_async_copy(out_ref, message_hbm.at[n, pl.ds(0, 3 * chunks)], out_sems.at[n])
+        for n in range(message_hbm.shape[0])
+    ]
     for copy in copies:
         copy.start()
     for copy in copies:
         copy.wait()
 
 
-def tile_copies(step, pairs, sems):
-    top, cols = tile_of(step)
-    out = []
-    for n, (hbm, tiles, outward) in enumerate(pairs):
-        far, near = hbm.at[pl.ds(top, TILE[0]), cols], tiles.at[step]
-        out.append(pltpu.make_async_copy(near if outward else far, far if outward else near, sems.at[n, step]))
-    return out
+def message_kernel(message_hbm, square_ref, out_hbm, total, sems):
+    total[...] = jnp.sum(square_ref[...], axis=0)
+    replicas, rows = out_hbm.shape[:2]
+    copies = [pltpu.make_async_copy(total, out_hbm.at[n, pl.ds(rows - 8, 8)], sems.at[n]) for n in range(replicas)]
+    for copy in copies:
+        copy.start()
+    for copy in copies:
+        copy.wait()
 
 
 def own_kernel(flag_ref, mom_hbm, grad_hbm, kept_ref, stacked_ref, u_hbm, v_hbm, mom, grad, u_out, v_out, in_sems, out_sems):
@@ -196,7 +208,7 @@
             copy.wait()
 
 
-def update_kernel(count, all_ref, u_hbm, v_hbm, rows_ref, cols_ref, mom_hbm, update_hbm, lists_a, lists_b, lists_h, lists_l, pooled,
+def update_kernel(count, all_ref, u_hbm, v_hbm, rows_ref, cols_ref, mom_hbm, update_hbm, lists_a, lists_b, lists_h, lists_l, pooled, columns,
                   u_ref, v_ref, mom_out, update_out, in_sems, mom_sems, update_sems):
     inward = [(u_hbm, u_ref, False), (v_hbm, v_ref, False)]
     for tile in range(4):
@@ -249,18 +261,25 @@
         out = dot_nt(jnp.concatenate([high, low], axis=0), hot)
         return out[:GROUP] + out[GROUP:]
 
-    def scatter_rows(part, slot):
-        for s in range(4):
-            for pair in range(2):
-                both = [scatter(4 * part + s, 2 * pair + n, slot) for n in range(2)]
-                pooled[part, s * GROUP:(s + 1) * GROUP, pair * LANES:(pair + 1) * LANES] = jnp.concatenate(both, axis=1)
-
-    def inverse(tile, part):
-        ph, plow = halves(pooled[part])
-        ch, cl = cols_ref[0], cols_ref[1]
-        yh, yl = halves(dot(ph, ch) + dot(plow, ch) + dot(ph, cl))
-        rh, rl = rows_ref[0], rows_ref[1]
-        update_out[tile, part] = dot(rh, yh) + dot(rh, yl) + dot(rl, yh)
+    def scatter_row(part, s, slot):
+        for pair in range(2):
+            both = [scatter(4 * part + s, 2 * pair + n, slot) for n in range(2)]
+            pooled[part, s * GROUP:(s + 1) * GROUP, pair * LANES:(pair + 1) * LANES] = jnp.concatenate(both, axis=1)
+
+    def inverse_steps(before, last, out):
+        table_c, table_r = cols_ref[...], rows_ref[...]
+        for n in range(2):
+            side = slice(n * LANES, (n + 1) * LANES)
+            x = dot(table_r, columns[last, n])
+            y = dot(jnp.concatenate(halves(pooled[before, :, side]), axis=1), table_c)
+            yield
+            update_out[out, last, side, :] = x[:LANES] + x[LANES:]
+            high, low = halves(y[:, :LANES] + y[:, LANES:])
+            for m in range(2):
+                here = slice(m * LANES, (m + 1) * LANES)
+                columns[before, m, :LANES, side] = high[here]
+                columns[before, m, LANES:, side] = low[here]
+            yield
 
     def update_copy(tile, part):
         top, cols = tile_of(tile)
@@ -271,31 +290,33 @@
         return tile_copies(tile, [(mom_hbm, mom_out, True)], mom_sems)[0]
 
     pooled[1] = jnp.zeros(pooled.shape[1:], F32)
+    columns[...] = jnp.zeros_like(columns)
     prepare(0, 0)
 
     def one(tile, carry):
         slot = tile % 2
         before = jnp.maximum(tile - 1, 0)
-        scatter_rows(0, slot)
-        inverse(before, 1)
-        scatter_rows(1, slot)
-        inverse(tile, 0)
+        for part in range(2):
+            for s, unused in enumerate(inverse_steps(1 - part, part, before)):
+                scatter_row(part, s, slot)
         for copy in tile_copies(tile, inward, in_sems):
             copy.wait()
         mom_out[tile] = u_ref[tile] + factor * v_ref[tile]
         prepare(jnp.minimum(tile + 1, 3), 1 - slot)
         mom_copy(tile).start()
-        update_copy(tile, 0).start()
 
         @pl.when(tile > 0)
         def _():
-            update_copy(before, 1).start()
+            for part in range(2):
+                update_copy(before, part).start()
 
         return carry
 
     lax.fori_loop(0, 4, one, 0)
-    inverse(3, 1)
-    update_copy(3, 1).start()
+    for part in range(2):
+        for unused in inverse_steps(1 - part, part, 3):
+            pass
+        update_copy(3, part).start()
     for tile in range(4):
         mom_copy(tile).wait()
         for part in range(2):
@@ -315,44 +336,52 @@
     far = lambda x: pltpu.with_memory_space_constraint(x, pltpu.HBM)
     near = lambda x: pltpu.with_memory_space_constraint(x, pltpu.VMEM)
 
-    squares, grad_near, mom_near, freq_rows = pl.pallas_call(
+    squares, grad_near, freq_rows = pl.pallas_call(
         square_kernel,
-        in_specs=[hbm] * 3,
-        out_specs=[hbm] + [vmem] * 3,
+        in_specs=[hbm] * 2,
+        out_specs=[hbm, vmem, vmem],
         out_shape=[
             pltpu.HBM((tensors, 8, LANES), F32),
             pltpu.VMEM(grad.shape, BF16),
-            pltpu.VMEM(mom.shape, F32),
             pltpu.VMEM((chunks, LANES), jnp.int32),
         ],
         scratch_shapes=[
             pltpu.VMEM(freq.shape, jnp.int32),
             pltpu.VMEM((tensors, 8, LANES), F32),
-            pltpu.SemaphoreType.DMA((3,)),
+            pltpu.SemaphoreType.DMA((2,)),
             pltpu.SemaphoreType.DMA((4,)),
         ],
         compiler_params=limit,
-    )(far(grad), far(mom), far(freq))
+    )(far(grad), far(freq))
     squares = lax.all_to_all(squares, "tensor", 0, 0)
 
-    kept = pl.pallas_call(
+    kept, message = pl.pallas_call(
         kept_kernel,
-        in_specs=[scalar] + [vmem] * 4,
-        out_specs=vmem,
-        out_shape=pltpu.VMEM((3 * chunks, LANES), F32),
-        scratch_shapes=[pltpu.VMEM((2, 2 * GROUP, 16 * LANES), BF16)],
+        in_specs=[scalar, hbm, vmem, vmem, vmem],
+        out_specs=[vmem, hbm],
+        out_shape=[
+            pltpu.VMEM((3 * chunks, LANES), F32),
+            pltpu.HBM((replicas, 3 * chunks + 8, LANES), F32),
+        ],
+        scratch_shapes=[
+            pltpu.VMEM((4,) + TILE, F32),
+            pltpu.VMEM((2, 2 * GROUP, 16 * LANES), BF16),
+            pltpu.SemaphoreType.DMA((1, 4)),
+            pltpu.SemaphoreType.DMA((replicas,)),
+        ],
         compiler_params=limit,
         cost_estimate=pl.CostEstimate(flops=2 * 10 ** 9, bytes_accessed=3 * 2 ** 20, transcendentals=0),
-    )(clip_flag, near(mom_near), near(grad_near), near(freq_rows), near(stacked))
+    )(clip_flag, far(mom), near(grad_near), near(freq_rows), near(stacked))
 
     message = pl.pallas_call(
         message_kernel,
-        in_specs=[vmem] * 2,
+        in_specs=[hbm, vmem],
         out_specs=hbm,
-        out_shape=pltpu.HBM((replicas, 3 * chunks + 8, LANES), F32),
-        scratch_shapes=[pltpu.VMEM((3 * chunks + 8, LANES), F32), pltpu.SemaphoreType.DMA((replicas,))],
+        out_shape=pltpu.HBM(message.shape, F32),
+        input_output_aliases={0: 0},
+        scratch_shapes=[pltpu.VMEM((8, LANES), F32), pltpu.SemaphoreType.DMA((replicas,))],
         compiler_params=limit,
-    )(near(kept), near(squares))
+    )(far(message), near(squares))
     everyone = lax.all_to_all(message, "replica", 0, 0)
 
     own_u, own_v = pl.pallas_call(
@@ -373,6 +402,7 @@
         scratch_shapes=[pltpu.VMEM((2, 4, 8, replicas * TOPK), t) for t in (jnp.int32, jnp.int32, F32, F32)]
         + [
             pltpu.VMEM((2, TILE[0] // 2, TILE[1]), F32),
+            pltpu.VMEM((2, 2, TILE[0] // 2, TILE[1]), BF16),
             pltpu.VMEM((4,) + TILE, F32),
             pltpu.VMEM((4,) + TILE, F32),
             pltpu.VMEM((4,) + TILE, F32),

time: 53.1 us -> 51.6 us (0.972)
  waiting for transfers between devices: 12.8 us -> 10.3 us
  local copies, waits for them, and re-layouts: 0.02 us -> 0.77 us
    all_to_all x1, waiting for transfers between devices: 4.71 us -> 2.21 us  [body(): squares = lax.all_to_all(squares, 'tensor', 0, 0)]
    pallas_call x3, Pallas kernels: 5.49 us -> 6.87 us  [the longest x1 4.16 us: body(): pl.pallas_call(kept_kernel, in_specs=[scalar, hbm, vmem, vmem, vmem], out...]
    pallas_call x1, Pallas kernels: 10.7 us -> 9.41 us  [body(): pl.pallas_call(lambda *refs: update_kernel(replicas * tensors * rows * co...]
    unnamed x6 -> x8, local copies, waits for them, and re-layouts: 0.02 us -> 0.77 us
  transfers between devices with their start and end apart: 2 -> 2, of which waited for: 2 -> 2; matrix products, arithmetic and copies ran while one was open for 0% -> 0% of each run, Pallas kernels for 14% -> 18%
where the time goes in v4:
time: 51.6 us; the launch traced here: 50.6 us
  Pallas kernels  21.4 us (41%)
  starting transfers between devices  16.8 us (33%)
  waiting for transfers between devices  10.3 us (20%)
  between operations  1.36 us (3%)
  local copies, waits for them, and re-layouts  0.77 us (1%)
    all_to_all x1, starting transfers between devices, body(): squares = lax.all_to_all(squares, 'tensor', 0, 0)  9.99 us
    pallas_call x1, Pallas kernels, body(): pl.pallas_call(lambda *refs: update_kernel(replicas * tensors * rows * co...  9.41 us
    all_to_all x1, waiting for transfers between devices, body(): everyone = lax.all_to_all(message, 'replica', 0, 0)  8.13 us
    all_to_all x1, starting transfers between devices, body(): everyone = lax.all_to_all(message, 'replica', 0, 0)  6.77 us
    pallas_call x1, Pallas kernels, body(): pl.pallas_call(own_kernel, in_specs=[scalar, hbm, hbm, vmem, vmem], out_s...  5.11 us
    pallas_call x1, Pallas kernels, body(): pl.pallas_call(kept_kernel, in_specs=[scalar, hbm, vmem, vmem, vmem], out...  4.16 us
    all_to_all x1, waiting for transfers between devices, body(): squares = lax.all_to_all(squares, 'tensor', 0, 0)  2.21 us
    pallas_call x1, Pallas kernels, body(): pl.pallas_call(square_kernel, in_specs=[hbm] * 2, out_specs=[hbm, vmem, v...  1.9 us
  transfers between devices with their start and end apart: 2, of which 2 were waited for; matrix products, arithmetic and copies ran while one was open for 0% of the time, Pallas kernels for 18%

profile of v4, /device:TPU:1, one launch (start us, length us, event | category | flops | bytes accessed | tf_op | source)
XLA Modules:
  0.0 50.6 jit_solution(15563415020681772139)
XLA Ops:
  0.6 1.9 %shard_map.86 = (f32[16,8,128]{2,1,0:T(8,128)}, bf16[1024,512]{1,0:T(8,128)(2,1)S(1)}, s32[32,128]{1,0:T(8,128)S(1)}) custom-call(bf16[1024,512]{1,0:T(8,128)(2,1)} %bitcast.4, s32[16,8,32]{2,1,0:T(8,128)} %bitcast.6), custom_call_target="tpu_custom_call" | custom-call | tf_op jit(solution)/shard_map/pallas_call | solution.py:339
  2.5 10.0 %all-to-all-start = ((f32[16,8,128]{2,1,0:T(8,128)}), f32[16,8,128]{2,1,0:T(8,128)S(1)}, u32[]{:S(2)}, u32[]{:S(2)}) async-start(f32[16,8,128]{2,1,0:T(8,128)} %get-tuple-element.14), calls=%async_computation | async-start | bytes 131072 | tf_op jit(solution)/shard_map/all_to_all | solution.py:356
  13.2 0.0 copy-start.2
  13.2 0.7 %copy-done.2 = bf16[128,64]{1,0:T(8,128)(2,1)S(1)} copy-done((bf16[128,64]{1,0:T(8,128)(2,1)S(1)}, bf16[128,64]{1,0:T(8,128)(2,1)}, u32[]{:S(2)}) %copy-start.2) | copy-done | bytes 16408
  13.9 4.2 %shard_map.87 = (f32[96,128]{1,0:T(8,128)S(1)}, f32[16,104,128]{2,1,0:T(8,128)}) custom-call(s32[1]{0:T(128)S(6)} %copy.11.flag_ref, f32[1024,512]{1,0:T(8,128)} %bitcast.7, bf16[1024,512]{1,0:T(8,128)(2,1)S(1)} %get-tuple-element.11.grad_ref, s32[32,128]{1,0:T(8,128)S(1)} %get-tuple-element.12.freq_rows, bf16[128,64]{1,0:T(8,128)(2,1)S(1)} %copy-done.2), custom_call_target="tpu_custom_call" | custom-call | flops 2000000000 | bytes 3145728 | tf_op jit(solution)/shard_map/pallas_call | solution.py:358
  18.1 0.0 copy-start.3
  18.1 2.2 %all-to-all-done.square_ref = f32[16,8,128]{2,1,0:T(8,128)S(1)} async-done(((f32[16,8,128]{2,1,0:T(8,128)}), f32[16,8,128]{2,1,0:T(8,128)S(1)}, u32[]{:S(2)}, u32[]{:S(2)}) %all-to-all-start) | async-done | bytes 65568 | tf_op jit(solution)/shard_map/all_to_all | solution.py:356
  20.3 0.8 %shard_map.88 = f32[16,104,128]{2,1,0:T(8,128)} custom-call(f32[16,104,128]{2,1,0:T(8,128)} %get-tuple-element.13.message_hbm, f32[16,8,128]{2,1,0:T(8,128)S(1)} %all-to-all-done.square_ref), custom_call_target="tpu_custom_call", output_to_operand_aliasing={{}: (0, {})} | custom-call | tf_op jit(solution)/shard_map/pallas_call | solution.py:376
  21.2 6.8 %all-to-all-start.1 = ((f32[16,104,128]{2,1,0:T(8,128)}), f32[16,104,128]{2,1,0:T(8,128)S(1)}, u32[]{:S(2)}, u32[]{:S(2)}) async-start(f32[16,104,128]{2,1,0:T(8,128)} %shard_map.88), calls=%async_computation.1 | async-start | bytes 1703936 | tf_op jit(solution)/shard_map/all_to_all | solution.py:385
  27.9 0.0 copy-done.3
  27.9 0.0 copy-start
  28.0 0.0 copy-start.1
  28.0 5.1 %shard_map.89 = (f32[1024,512]{1,0:T(8,128)}, f32[1024,512]{1,0:T(8,128)}) custom-call(s32[1]{0:T(128)S(6)} %copy.11.flag_ref, f32[1024,512]{1,0:T(8,128)} %bitcast.8, bf16[1024,512]{1,0:T(8,128)(2,1)} %bitcast.5, f32[96,128]{1,0:T(8,128)S(1)} %get-tuple-element.15.kept_ref, bf16[128,64]{1,0:T(8,128)(2,1)S(1)} %copy-done.3), custom_call_target="tpu_custom_call" | custom-call | flops 2000000000 | bytes 7340032 | tf_op jit(solution)/shard_map/pallas_call | solution.py:387
  33.1 8.1 %all-to-all-done.1.refs_0_ = f32[16,104,128]{2,1,0:T(8,128)S(1)} async-done(((f32[16,104,128]{2,1,0:T(8,128)}), f32[16,104,128]{2,1,0:T(8,128)S(1)}, u32[]{:S(2)}, u32[]{:S(2)}) %all-to-all-start.1) | async-done | bytes 852000 | tf_op jit(solution)/shard_map/all_to_all | solution.py:385
  41.2 0.0 copy-done
  41.2 0.0 copy-done.1
  41.2 9.4 %shard_map.90 = (f32[1024,512]{1,0:T(8,128)}, f32[1024,512]{1,0:T(8,128)}) custom-call(f32[16,104,128]{2,1,0:T(8,128)S(1)} %all-to-all-done.1.refs_0_, f32[1024,512]{1,0:T(8,128)} %get-tuple-element.16.refs_1_, f32[1024,512]{1,0:T(8,128)} %get-tuple-element.17.refs_2_, bf16[256,256]{1,0:T(8,128)(2,1)S(1)} %copy-done.1, bf16[256,256]{1,0:T(8,128)(2,1)S(1)} %copy-done), custom_call_target="tpu_custom_call" | custom-call | tf_op jit(solution)/shard_map/pallas_call | solution.py:397
Async XLA Ops:
  2.5 17.8 %all-to-all-start = ((f32[16,8,128]{2,1,0:T(8,128)}), f32[16,8,128]{2,1,0:T(8,128)S(1)}, u32[]{:S(2)}, u32[]{:S(2)}) async-start(f32[16,8,128]{2,1,0:T(8,128)} %get-tuple-element.14), calls=%async_computation | async-start | bytes 131072 | tf_op jit(solution)/shard_map/all_to_all | solution.py:356
  13.2 0.8 %copy-start.2 = (bf16[128,64]{1,0:T(8,128)(2,1)S(1)}, bf16[128,64]{1,0:T(8,128)(2,1)}, u32[]{:S(2)}) copy-start(bf16[128,64]{1,0:T(8,128)(2,1)} %constant.6.clone.stacked_ref) | copy-start | bytes 49156
  18.1 9.8 %copy-start.3 = (bf16[128,64]{1,0:T(8,128)(2,1)S(1)}, bf16[128,64]{1,0:T(8,128)(2,1)}, u32[]{:S(2)}) copy-start(bf16[128,64]{1,0:T(8,128)(2,1)} %constant.6.clone.stacked_ref) | copy-start | bytes 49156
  21.2 20.1 %all-to-all-start.1 = ((f32[16,104,128]{2,1,0:T(8,128)}), f32[16,104,128]{2,1,0:T(8,128)S(1)}, u32[]{:S(2)}, u32[]{:S(2)}) async-start(f32[16,104,128]{2,1,0:T(8,128)} %shard_map.88), calls=%async_computation.1 | async-start | bytes 1703936 | tf_op jit(solution)/shard_map/all_to_all | solution.py:385
  27.9 13.3 %copy-start = (bf16[256,256]{1,0:T(8,128)(2,1)S(1)}, bf16[256,256]{1,0:T(8,128)(2,1)}, u32[]{:S(2)}) copy-start(bf16[256,256]{1,0:T(8,128)(2,1)} %constant.8.clone.refs_4_) | copy-start | bytes 393220
  28.0 13.3 %copy-start.1 = (bf16[256,256]{1,0:T(8,128)(2,1)S(1)}, bf16[256,256]{1,0:T(8,128)(2,1)}, u32[]{:S(2)}) copy-start(bf16[256,256]{1,0:T(8,128)(2,1)} %constant.7.clone.refs_3_) | copy-start | bytes 393220

commit v5 on v4

--- a/solution.py
+++ b/solution.py
@@ -241,23 +241,26 @@
                 fs.append(all_ref[r, pl.ds(2 * chunks + at, 8), :])
             for m in range(4):
                 k = regroup(ks, m)
-                f = regroup(fs, m).astype(jnp.int32)
+                f = regroup(fs, m)
+                a = jnp.floor(f * (1.0 / GROUP))
                 high = k.astype(BF16).astype(F32)
                 place = slice(group * LANES, (group + 1) * LANES)
-                lists_a[slot, m, :, place] = lax.shift_right_logical(f, 6)
-                lists_b[slot, m, :, place] = lax.bitwise_and(f, GROUP - 1)
+                lists_a[slot, m, :, place] = a
+                lists_b[slot, m, :, place] = f - a * GROUP
                 lists_h[slot, m, :, place] = high
                 lists_l[slot, m, :, place] = k - high
 
     items = replicas * TOPK
-    place = lax.broadcasted_iota(jnp.int32, (GROUP, items), 0)
+    place = lax.broadcasted_iota(jnp.int32, (GROUP, items), 0).astype(F32).astype(BF16)
+    zero = jnp.zeros((), BF16)
 
     def scatter(s, m, slot):
         here = slice(s, s + 1)
-        hit = place == lists_a[slot, m, here, :]
-        high = jnp.where(hit, lists_h[slot, m, here, :], 0.0).astype(BF16)
-        low = jnp.where(hit, lists_l[slot, m, here, :], 0.0).astype(BF16)
-        hot = jnp.where(place == lists_b[slot, m, here, :], 1.0, 0.0).astype(BF16)
+        a, b, h, l = (x[slot, m, here, :].astype(BF16) for x in (lists_a, lists_b, lists_h, lists_l))
+        hit = place == a
+        high = jnp.where(hit, h, zero)
+        low = jnp.where(hit, l, zero)
+        hot = jnp.where(place == b, jnp.ones((), BF16), zero)
         out = dot_nt(jnp.concatenate([high, low], axis=0), hot)
         return out[:GROUP] + out[GROUP:]
 
@@ -266,14 +269,17 @@
             both = [scatter(4 * part + s, 2 * pair + n, slot) for n in range(2)]
             pooled[part, s * GROUP:(s + 1) * GROUP, pair * LANES:(pair + 1) * LANES] = jnp.concatenate(both, axis=1)
 
-    def inverse_steps(before, last, out):
+    def inverse_steps(before, last, out, final=False):
         table_c, table_r = cols_ref[...], rows_ref[...]
         for n in range(2):
             side = slice(n * LANES, (n + 1) * LANES)
             x = dot(table_r, columns[last, n])
-            y = dot(jnp.concatenate(halves(pooled[before, :, side]), axis=1), table_c)
+            if not final:
+                y = dot(jnp.concatenate(halves(pooled[before, :, side]), axis=1), table_c)
             yield
             update_out[out, last, side, :] = x[:LANES] + x[LANES:]
+            if final:
+                continue
             high, low = halves(y[:, :LANES] + y[:, LANES:])
             for m in range(2):
                 here = slice(m * LANES, (m + 1) * LANES)
@@ -296,13 +302,13 @@
     def one(tile, carry):
         slot = tile % 2
         before = jnp.maximum(tile - 1, 0)
+        prepare(jnp.minimum(tile + 1, 3), 1 - slot)
         for part in range(2):
             for s, unused in enumerate(inverse_steps(1 - part, part, before)):
                 scatter_row(part, s, slot)
         for copy in tile_copies(tile, inward, in_sems):
             copy.wait()
         mom_out[tile] = u_ref[tile] + factor * v_ref[tile]
-        prepare(jnp.minimum(tile + 1, 3), 1 - slot)
         mom_copy(tile).start()
 
         @pl.when(tile > 0)
@@ -314,7 +320,7 @@
 
     lax.fori_loop(0, 4, one, 0)
     for part in range(2):
-        for unused in inverse_steps(1 - part, part, 3):
+        for unused in inverse_steps(1 - part, part, 3, final=part == 1):
             pass
         update_copy(3, part).start()
     for tile in range(4):
@@ -399,7 +405,7 @@
         in_specs=[vmem, hbm, hbm, vmem, vmem],
         out_specs=[hbm] * 2,
         out_shape=[jax.ShapeDtypeStruct((rows, cols), F32)] * 2,
-        scratch_shapes=[pltpu.VMEM((2, 4, 8, replicas * TOPK), t) for t in (jnp.int32, jnp.int32, F32, F32)]
+        scratch_shapes=[pltpu.VMEM((2, 4, 8, replicas * TOPK), t) for t in (F32,) * 4]
         + [
             pltpu.VMEM((2, TILE[0] // 2, TILE[1]), F32),
             pltpu.VMEM((2, 2, TILE[0] // 2, TILE[1]), BF16),

time: 51.6 us -> 50.7 us (0.983)
  Pallas kernels: 21.4 us -> 20.6 us
    pallas_call x1, Pallas kernels: 9.41 us -> 8.59 us  [body(): pl.pallas_call(lambda *refs: update_kernel(replicas * tensors * rows * co...]
  transfers between devices with their start and end apart: 2 -> 2, of which waited for: 2 -> 2; matrix products, arithmetic and copies ran while one was open for 0% -> 0% of each run, Pallas kernels for 18% -> 19%
where the time goes in v5:
time: 50.7 us; the launch traced here: 49.8 us
  Pallas kernels  20.6 us (41%)
  starting transfers between devices  16.8 us (33%)
  waiting for transfers between devices  10.3 us (20%)
  between operations  1.36 us (3%)
  local copies, waits for them, and re-layouts  0.77 us (2%)
    all_to_all x1, starting transfers between devices, body(): squares = lax.all_to_all(squares, 'tensor', 0, 0)  9.99 us
    pallas_call x1, Pallas kernels, body(): pl.pallas_call(lambda *refs: update_kernel(replicas * tensors * rows * co...  8.59 us
    all_to_all x1, waiting for transfers between devices, body(): everyone = lax.all_to_all(message, 'replica', 0, 0)  8.13 us
    all_to_all x1, starting transfers between devices, body(): everyone = lax.all_to_all(message, 'replica', 0, 0)  6.77 us
    pallas_call x1, Pallas kernels, body(): pl.pallas_call(own_kernel, in_specs=[scalar, hbm, hbm, vmem, vmem], out_s...  5.11 us
    pallas_call x1, Pallas kernels, body(): pl.pallas_call(kept_kernel, in_specs=[scalar, hbm, vmem, vmem, vmem], out...  4.16 us
    all_to_all x1, waiting for transfers between devices, body(): squares = lax.all_to_all(squares, 'tensor', 0, 0)  2.21 us
    pallas_call x1, Pallas kernels, body(): pl.pallas_call(square_kernel, in_specs=[hbm] * 2, out_specs=[hbm, vmem, v...  1.9 us
  transfers between devices with their start and end apart: 2, of which 2 were waited for; matrix products, arithmetic and copies ran while one was open for 0% of the time, Pallas kernels for 19%

profile of v5, /device:TPU:1, one launch (start us, length us, event | category | flops | bytes accessed | tf_op | source)
XLA Modules:
  0.0 49.8 jit_solution(10966354544994960020)
XLA Ops:
  0.6 1.9 %shard_map.86 = (f32[16,8,128]{2,1,0:T(8,128)}, bf16[1024,512]{1,0:T(8,128)(2,1)S(1)}, s32[32,128]{1,0:T(8,128)S(1)}) custom-call(bf16[1024,512]{1,0:T(8,128)(2,1)} %bitcast.4, s32[16,8,32]{2,1,0:T(8,128)} %bitcast.6), custom_call_target="tpu_custom_call" | custom-call | tf_op jit(solution)/shard_map/pallas_call | solution.py:345
  2.5 10.0 %all-to-all-start = ((f32[16,8,128]{2,1,0:T(8,128)}), f32[16,8,128]{2,1,0:T(8,128)S(1)}, u32[]{:S(2)}, u32[]{:S(2)}) async-start(f32[16,8,128]{2,1,0:T(8,128)} %get-tuple-element.14), calls=%async_computation | async-start | bytes 131072 | tf_op jit(solution)/shard_map/all_to_all | solution.py:362
  13.2 0.0 copy-start.2
  13.2 0.7 %copy-done.2 = bf16[128,64]{1,0:T(8,128)(2,1)S(1)} copy-done((bf16[128,64]{1,0:T(8,128)(2,1)S(1)}, bf16[128,64]{1,0:T(8,128)(2,1)}, u32[]{:S(2)}) %copy-start.2) | copy-done | bytes 16408
  13.9 4.2 %shard_map.87 = (f32[96,128]{1,0:T(8,128)S(1)}, f32[16,104,128]{2,1,0:T(8,128)}) custom-call(s32[1]{0:T(128)S(6)} %copy.11.flag_ref, f32[1024,512]{1,0:T(8,128)} %bitcast.7, bf16[1024,512]{1,0:T(8,128)(2,1)S(1)} %get-tuple-element.11.grad_ref, s32[32,128]{1,0:T(8,128)S(1)} %get-tuple-element.12.freq_rows, bf16[128,64]{1,0:T(8,128)(2,1)S(1)} %copy-done.2), custom_call_target="tpu_custom_call" | custom-call | flops 2000000000 | bytes 3145728 | tf_op jit(solution)/shard_map/pallas_call | solution.py:364
  18.1 0.0 copy-start.3
  18.1 2.2 %all-to-all-done.square_ref = f32[16,8,128]{2,1,0:T(8,128)S(1)} async-done(((f32[16,8,128]{2,1,0:T(8,128)}), f32[16,8,128]{2,1,0:T(8,128)S(1)}, u32[]{:S(2)}, u32[]{:S(2)}) %all-to-all-start) | async-done | bytes 65568 | tf_op jit(solution)/shard_map/all_to_all | solution.py:362
  20.3 0.8 %shard_map.88 = f32[16,104,128]{2,1,0:T(8,128)} custom-call(f32[16,104,128]{2,1,0:T(8,128)} %get-tuple-element.13.message_hbm, f32[16,8,128]{2,1,0:T(8,128)S(1)} %all-to-all-done.square_ref), custom_call_target="tpu_custom_call", output_to_operand_aliasing={{}: (0, {})} | custom-call | tf_op jit(solution)/shard_map/pallas_call | solution.py:382
  21.2 6.8 %all-to-all-start.1 = ((f32[16,104,128]{2,1,0:T(8,128)}), f32[16,104,128]{2,1,0:T(8,128)S(1)}, u32[]{:S(2)}, u32[]{:S(2)}) async-start(f32[16,104,128]{2,1,0:T(8,128)} %shard_map.88), calls=%async_computation.1 | async-start | bytes 1703936 | tf_op jit(solution)/shard_map/all_to_all | solution.py:391
  27.9 0.0 copy-done.3
  27.9 0.0 copy-start
  28.0 0.0 copy-start.1
  28.0 5.1 %shard_map.89 = (f32[1024,512]{1,0:T(8,128)}, f32[1024,512]{1,0:T(8,128)}) custom-call(s32[1]{0:T(128)S(6)} %copy.11.flag_ref, f32[1024,512]{1,0:T(8,128)} %bitcast.8, bf16[1024,512]{1,0:T(8,128)(2,1)} %bitcast.5, f32[96,128]{1,0:T(8,128)S(1)} %get-tuple-element.15.kept_ref, bf16[128,64]{1,0:T(8,128)(2,1)S(1)} %copy-done.3), custom_call_target="tpu_custom_call" | custom-call | flops 2000000000 | bytes 7340032 | tf_op jit(solution)/shard_map/pallas_call | solution.py:393
  33.1 8.1 %all-to-all-done.1.refs_0_ = f32[16,104,128]{2,1,0:T(8,128)S(1)} async-done(((f32[16,104,128]{2,1,0:T(8,128)}), f32[16,104,128]{2,1,0:T(8,128)S(1)}, u32[]{:S(2)}, u32[]{:S(2)}) %all-to-all-start.1) | async-done | bytes 852000 | tf_op jit(solution)/shard_map/all_to_all | solution.py:391
  41.2 0.0 copy-done
  41.2 0.0 copy-done.1
  41.2 8.6 %shard_map.90 = (f32[1024,512]{1,0:T(8,128)}, f32[1024,512]{1,0:T(8,128)}) custom-call(f32[16,104,128]{2,1,0:T(8,128)S(1)} %all-to-all-done.1.refs_0_, f32[1024,512]{1,0:T(8,128)} %get-tuple-element.16.refs_1_, f32[1024,512]{1,0:T(8,128)} %get-tuple-element.17.refs_2_, bf16[256,256]{1,0:T(8,128)(2,1)S(1)} %copy-done.1, bf16[256,256]{1,0:T(8,128)(2,1)S(1)} %copy-done), custom_call_target="tpu_custom_call" | custom-call | tf_op jit(solution)/shard_map/pallas_call | solution.py:403
Async XLA Ops:
  2.5 17.8 %all-to-all-start = ((f32[16,8,128]{2,1,0:T(8,128)}), f32[16,8,128]{2,1,0:T(8,128)S(1)}, u32[]{:S(2)}, u32[]{:S(2)}) async-start(f32[16,8,128]{2,1,0:T(8,128)} %get-tuple-element.14), calls=%async_computation | async-start | bytes 131072 | tf_op jit(solution)/shard_map/all_to_all | solution.py:362
  13.2 0.8 %copy-start.2 = (bf16[128,64]{1,0:T(8,128)(2,1)S(1)}, bf16[128,64]{1,0:T(8,128)(2,1)}, u32[]{:S(2)}) copy-start(bf16[128,64]{1,0:T(8,128)(2,1)} %constant.6.clone.stacked_ref) | copy-start | bytes 49156
  18.1 9.8 %copy-start.3 = (bf16[128,64]{1,0:T(8,128)(2,1)S(1)}, bf16[128,64]{1,0:T(8,128)(2,1)}, u32[]{:S(2)}) copy-start(bf16[128,64]{1,0:T(8,128)(2,1)} %constant.6.clone.stacked_ref) | copy-start | bytes 49156
  21.2 20.1 %all-to-all-start.1 = ((f32[16,104,128]{2,1,0:T(8,128)}), f32[16,104,128]{2,1,0:T(8,128)S(1)}, u32[]{:S(2)}, u32[]{:S(2)}) async-start(f32[16,104,128]{2,1,0:T(8,128)} %shard_map.88), calls=%async_computation.1 | async-start | bytes 1703936 | tf_op jit(solution)/shard_map/all_to_all | solution.py:391
  27.9 13.3 %copy-start = (bf16[256,256]{1,0:T(8,128)(2,1)S(1)}, bf16[256,256]{1,0:T(8,128)(2,1)}, u32[]{:S(2)}) copy-start(bf16[256,256]{1,0:T(8,128)(2,1)} %constant.8.clone.refs_4_) | copy-start | bytes 393220
  28.0 13.3 %copy-start.1 = (bf16[256,256]{1,0:T(8,128)(2,1)S(1)}, bf16[256,256]{1,0:T(8,128)(2,1)}, u32[]{:S(2)}) copy-start(bf16[256,256]{1,0:T(8,128)(2,1)} %constant.7.clone.refs_3_) | copy-start | bytes 393220

commit v6 on v5

--- a/solution.py
+++ b/solution.py
@@ -329,6 +329,12 @@
             update_copy(tile, part).wait()
 
 
+def spread(copies, axis, minor):
+    size = lax.axis_size(axis)
+    order = sorted(range(size), key=lambda i: (i % minor, i), reverse=True)
+    return lax.all_to_all(copies, axis, 0, 0, axis_index_groups=[order])
+
+
 def body(momentum, gradient, kept_freq, clip_flag):
     replicas, tensors = lax.axis_size("replica"), lax.axis_size("tensor")
     mom, grad, freq = momentum[0], gradient[0], kept_freq[0]
@@ -359,7 +365,7 @@
         ],
         compiler_params=limit,
     )(far(grad), far(freq))
-    squares = lax.all_to_all(squares, "tensor", 0, 0)
+    squares = spread(squares, "tensor", 2)
 
     kept, message = pl.pallas_call(
         kept_kernel,
@@ -388,7 +394,7 @@
         scratch_shapes=[pltpu.VMEM((8, LANES), F32), pltpu.SemaphoreType.DMA((replicas,))],
         compiler_params=limit,
     )(far(message), near(squares))
-    everyone = lax.all_to_all(message, "replica", 0, 0)
+    everyone = spread(message, "replica", 4)
 
     own_u, own_v = pl.pallas_call(
         own_kernel,

time: 50.7 us -> 46.9 us (0.925); the launches traced: 49.8 us -> 46.5 us
  waiting for transfers between devices: 10.3 us -> 5.45 us
  starting transfers between devices: 16.8 us -> 18.3 us
    all_to_all x2, waiting for transfers between devices: 10.3 us -> 5.45 us  [spread(): return lax.all_to_all(copies, axis, 0, 0, axis_index_groups=[order])]
    all_to_all x2, starting transfers between devices: 16.8 us -> 18.3 us  [spread(): return lax.all_to_all(copies, axis, 0, 0, axis_index_groups=[order])]
  transfers between devices with their start and end apart: 2 -> 2, of which waited for: 2 -> 1; matrix products, arithmetic and copies ran while one was open for 0% -> 0% of each run, Pallas kernels for 19% -> 20%
where the time goes in v6:
time: 46.9 us; the launch traced here: 46.5 us
  Pallas kernels  20.6 us (44%)
  starting transfers between devices  18.3 us (39%)
  waiting for transfers between devices  5.45 us (12%)
  between operations  1.36 us (3%)
  local copies, waits for them, and re-layouts  0.77 us (2%)
    all_to_all x2, starting transfers between devices, spread(): return lax.all_to_all(copies, axis, 0, 0, axis_index_groups=[order])  18.3 us
    pallas_call x1, Pallas kernels, body(): pl.pallas_call(lambda *refs: update_kernel(replicas * tensors * rows * co...  8.59 us
    all_to_all x2, waiting for transfers between devices, spread(): return lax.all_to_all(copies, axis, 0, 0, axis_index_groups=[order])  5.45 us
    pallas_call x1, Pallas kernels, body(): pl.pallas_call(own_kernel, in_specs=[scalar, hbm, hbm, vmem, vmem], out_s...  5.14 us
    pallas_call x1, Pallas kernels, body(): pl.pallas_call(kept_kernel, in_specs=[scalar, hbm, vmem, vmem, vmem], out...  4.18 us
    pallas_call x1, Pallas kernels, body(): pl.pallas_call(square_kernel, in_specs=[hbm] * 2, out_specs=[hbm, vmem, v...  1.9 us
  transfers between devices with their start and end apart: 2, of which 1 were waited for; matrix products, arithmetic and copies ran while one was open for 0% of the time, Pallas kernels for 20%

profile of v6, /device:TPU:1, one launch (start us, length us, event | category | flops | bytes accessed | tf_op | source)
XLA Modules:
  0.0 46.5 jit_solution(12047109571228651520)
XLA Ops:
  0.6 1.9 %shard_map.86 = (f32[16,8,128]{2,1,0:T(8,128)}, bf16[1024,512]{1,0:T(8,128)(2,1)S(1)}, s32[32,128]{1,0:T(8,128)S(1)}) custom-call(bf16[1024,512]{1,0:T(8,128)(2,1)} %bitcast.4, s32[16,8,32]{2,1,0:T(8,128)} %bitcast.6), custom_call_target="tpu_custom_call" | custom-call | tf_op jit(solution)/shard_map/pallas_call | solution.py:351
  2.5 9.9 %all-to-all-start = ((f32[16,8,128]{2,1,0:T(8,128)}), f32[16,8,128]{2,1,0:T(8,128)S(1)}, u32[]{:S(2)}, u32[]{:S(2)}) async-start(f32[16,8,128]{2,1,0:T(8,128)} %get-tuple-element.14), calls=%async_computation | async-start | bytes 131072 | tf_op jit(solution)/shard_map/all_to_all | solution.py:335
  13.1 0.0 copy-start.2
  13.1 0.7 %copy-done.2 = bf16[128,64]{1,0:T(8,128)(2,1)S(1)} copy-done((bf16[128,64]{1,0:T(8,128)(2,1)S(1)}, bf16[128,64]{1,0:T(8,128)(2,1)}, u32[]{:S(2)}) %copy-start.2) | copy-done | bytes 16408
  13.8 4.2 %shard_map.87 = (f32[96,128]{1,0:T(8,128)S(1)}, f32[16,104,128]{2,1,0:T(8,128)}) custom-call(s32[1]{0:T(128)S(6)} %copy.11.flag_ref, f32[1024,512]{1,0:T(8,128)} %bitcast.7, bf16[1024,512]{1,0:T(8,128)(2,1)S(1)} %get-tuple-element.11.grad_ref, s32[32,128]{1,0:T(8,128)S(1)} %get-tuple-element.12.freq_rows, bf16[128,64]{1,0:T(8,128)(2,1)S(1)} %copy-done.2), custom_call_target="tpu_custom_call" | custom-call | flops 2000000000 | bytes 3145728 | tf_op jit(solution)/shard_map/pallas_call | solution.py:370
  18.0 0.0 copy-start.3
  18.0 0.0 all-to-all-done.square_ref
  18.0 0.8 %shard_map.88 = f32[16,104,128]{2,1,0:T(8,128)} custom-call(f32[16,104,128]{2,1,0:T(8,128)} %get-tuple-element.13.message_hbm, f32[16,8,128]{2,1,0:T(8,128)S(1)} %all-to-all-done.square_ref), custom_call_target="tpu_custom_call", output_to_operand_aliasing={{}: (0, {})} | custom-call | tf_op jit(solution)/shard_map/pallas_call | solution.py:388
  18.9 8.4 %all-to-all-start.1 = ((f32[16,104,128]{2,1,0:T(8,128)}), f32[16,104,128]{2,1,0:T(8,128)S(1)}, u32[]{:S(2)}, u32[]{:S(2)}) async-start(f32[16,104,128]{2,1,0:T(8,128)} %shard_map.88), calls=%async_computation.1 | async-start | bytes 1703936 | tf_op jit(solution)/shard_map/all_to_all | solution.py:335
  27.3 0.0 copy-done.3
  27.3 0.0 copy-start
  27.3 0.0 copy-start.1
  27.3 5.1 %shard_map.89 = (f32[1024,512]{1,0:T(8,128)}, f32[1024,512]{1,0:T(8,128)}) custom-call(s32[1]{0:T(128)S(6)} %copy.11.flag_ref, f32[1024,512]{1,0:T(8,128)} %bitcast.8, bf16[1024,512]{1,0:T(8,128)(2,1)} %bitcast.5, f32[96,128]{1,0:T(8,128)S(1)} %get-tuple-element.15.kept_ref, bf16[128,64]{1,0:T(8,128)(2,1)S(1)} %copy-done.3), custom_call_target="tpu_custom_call" | custom-call | flops 2000000000 | bytes 7340032 | tf_op jit(solution)/shard_map/pallas_call | solution.py:399
  32.5 5.4 %all-to-all-done.1.refs_0_ = f32[16,104,128]{2,1,0:T(8,128)S(1)} async-done(((f32[16,104,128]{2,1,0:T(8,128)}), f32[16,104,128]{2,1,0:T(8,128)S(1)}, u32[]{:S(2)}, u32[]{:S(2)}) %all-to-all-start.1) | async-done | bytes 852000 | tf_op jit(solution)/shard_map/all_to_all | solution.py:335
  37.9 0.0 copy-done
  37.9 0.0 copy-done.1
  37.9 8.6 %shard_map.90 = (f32[1024,512]{1,0:T(8,128)}, f32[1024,512]{1,0:T(8,128)}) custom-call(f32[16,104,128]{2,1,0:T(8,128)S(1)} %all-to-all-done.1.refs_0_, f32[1024,512]{1,0:T(8,128)} %get-tuple-element.16.refs_1_, f32[1024,512]{1,0:T(8,128)} %get-tuple-element.17.refs_2_, bf16[256,256]{1,0:T(8,128)(2,1)S(1)} %copy-done.1, bf16[256,256]{1,0:T(8,128)(2,1)S(1)} %copy-done), custom_call_target="tpu_custom_call" | custom-call | tf_op jit(solution)/shard_map/pallas_call | solution.py:409
Async XLA Ops:
  2.5 15.5 %all-to-all-start = ((f32[16,8,128]{2,1,0:T(8,128)}), f32[16,8,128]{2,1,0:T(8,128)S(1)}, u32[]{:S(2)}, u32[]{:S(2)}) async-start(f32[16,8,128]{2,1,0:T(8,128)} %get-tuple-element.14), calls=%async_computation | async-start | bytes 131072 | tf_op jit(solution)/shard_map/all_to_all | solution.py:335
  13.1 0.8 %copy-start.2 = (bf16[128,64]{1,0:T(8,128)(2,1)S(1)}, bf16[128,64]{1,0:T(8,128)(2,1)}, u32[]{:S(2)}) copy-start(bf16[128,64]{1,0:T(8,128)(2,1)} %constant.6.clone.stacked_ref) | copy-start | bytes 49156
  18.0 9.3 %copy-start.3 = (bf16[128,64]{1,0:T(8,128)(2,1)S(1)}, bf16[128,64]{1,0:T(8,128)(2,1)}, u32[]{:S(2)}) copy-start(bf16[128,64]{1,0:T(8,128)(2,1)} %constant.6.clone.stacked_ref) | copy-start | bytes 49156
  18.9 19.1 %all-to-all-start.1 = ((f32[16,104,128]{2,1,0:T(8,128)}), f32[16,104,128]{2,1,0:T(8,128)S(1)}, u32[]{:S(2)}, u32[]{:S(2)}) async-start(f32[16,104,128]{2,1,0:T(8,128)} %shard_map.88), calls=%async_computation.1 | async-start | bytes 1703936 | tf_op jit(solution)/shard_map/all_to_all | solution.py:335
  27.3 10.6 %copy-start = (bf16[256,256]{1,0:T(8,128)(2,1)S(1)}, bf16[256,256]{1,0:T(8,128)(2,1)}, u32[]{:S(2)}) copy-start(bf16[256,256]{1,0:T(8,128)(2,1)} %constant.8.clone.refs_4_) | copy-start | bytes 393220
  27.3 10.6 %copy-start.1 = (bf16[256,256]{1,0:T(8,128)(2,1)S(1)}, bf16[256,256]{1,0:T(8,128)(2,1)}, u32[]{:S(2)}) copy-start(bf16[256,256]{1,0:T(8,128)(2,1)} %constant.7.clone.refs_3_) | copy-start | bytes 393220

commit v7 on v6

--- a/solution.py
+++ b/solution.py
@@ -51,7 +51,8 @@
     return lax.dot_general(a, b, (((1,), (1,)), ((), ())), preferred_element_type=F32)
 
 
-def square_kernel(grad_hbm, freq_hbm, square_hbm, grad_ref, freq_rows, freq_ref, squares, sems, grad_sems):
+def square_kernel(grad_hbm, mom_hbm, freq_hbm, stacked_hbm, square_hbm, grad_ref, mom_ref, freq_rows, stacked_ref, freq_ref, squares, sems,
+                  grad_sems):
     pieces = 4
     rows = grad_ref.shape[0] // pieces
     small = pltpu.make_async_copy(freq_hbm, freq_ref, sems.at[0])
@@ -59,7 +60,11 @@
     for n in range(pieces):
         here = pl.ds(n * rows, rows)
         large.append(pltpu.make_async_copy(grad_hbm.at[here], grad_ref.at[here], grad_sems.at[n]))
-    for copy in large + [small]:
+    rest = [
+        pltpu.make_async_copy(stacked_hbm, stacked_ref, sems.at[2]),
+        pltpu.make_async_copy(mom_hbm, mom_ref, sems.at[3]),
+    ]
+    for copy in large + [small] + rest:
         copy.start()
     part = jnp.zeros((8, LANES), F32)
     for n, copy in enumerate(large):
@@ -68,6 +73,7 @@
         g = g * g
         g = g.reshape(-1, 8, g.shape[1]).sum(axis=0)
         part += sum(g[:, m * LANES:(m + 1) * LANES] for m in range(g.shape[1] // LANES))
+    part = jnp.sum(part, axis=0, keepdims=True)
     for n in range(squares.shape[0]):
         squares[n] = part
     result = pltpu.make_async_copy(squares, square_hbm, sems.at[1])
@@ -76,6 +82,8 @@
     for col in range(2):
         freq_rows[16 * col:16 * col + 16, :] = jnp.concatenate([freq_ref[:, 4 * col + m, :] for m in range(4)], axis=1)
     result.wait()
+    for copy in rest:
+        copy.wait()
 
 
 def table_rows(freqs, stacked):
@@ -113,11 +121,7 @@
     return out
 
 
-def kept_kernel(flag_ref, mom_hbm, grad_ref, freq_rows, stacked_ref, out_ref, message_hbm, mom, table, in_sems, out_sems):
-    inward = [(mom_hbm, mom, False)]
-    for step in range(4):
-        for copy in tile_copies(step, inward, in_sems):
-            copy.start()
+def kept_kernel(flag_ref, mom_ref, grad_ref, freq_rows, stacked_ref, out_ref, message_hbm, table, out_sems):
     flag = (flag_ref[0] == 1).astype(F32)
     stacked = stacked_ref[...]
     chunks = freq_rows.shape[0]
@@ -128,15 +132,13 @@
         later = pl.multiple_of(jnp.minimum(step + 1, 3) * 8, 8)
         top, cols = tile_of(step)
         freqs = freq_rows[pl.ds(at, 8), :]
-        for copy in tile_copies(step, inward, in_sems):
-            copy.wait()
         us, vs = [], []
         for s in range(8):
-            rows = slice(s * GROUP, (s + 1) * GROUP)
+            rows = pl.ds(top + s * GROUP, GROUP)
             ah, al, bh, bl = parts(table.at[step % 2], s)
             weights = jnp.concatenate([diagonal(bh), diagonal(bl)], axis=1)
-            xh, xl = halves(mom[step, rows, :])
-            y = dot(jnp.concatenate([xh, xl, grad_ref[pl.ds(top + s * GROUP, GROUP), cols]], axis=0), weights)
+            xh, xl = halves(mom_ref[rows, cols])
+            y = dot(jnp.concatenate([xh, xl, grad_ref[rows, cols]], axis=0), weights)
             y = y[:, :LANES] + y[:, LANES:]
             a = ah.astype(F32) + al.astype(F32)
             km = jnp.sum((y[:GROUP] + y[GROUP:2 * GROUP]) * a, axis=0, keepdims=True)
@@ -161,7 +163,8 @@
 
 
 def message_kernel(message_hbm, square_ref, out_hbm, total, sems):
-    total[...] = jnp.sum(square_ref[...], axis=0)
+    total[...] = jnp.zeros_like(total)
+    total[:1, :] = jnp.sum(square_ref[...], axis=0)
     replicas, rows = out_hbm.shape[:2]
     copies = [pltpu.make_async_copy(total, out_hbm.at[n, pl.ds(rows - 8, 8)], sems.at[n]) for n in range(replicas)]
     for copy in copies:
@@ -348,42 +351,42 @@
     far = lambda x: pltpu.with_memory_space_constraint(x, pltpu.HBM)
     near = lambda x: pltpu.with_memory_space_constraint(x, pltpu.VMEM)
 
-    squares, grad_near, freq_rows = pl.pallas_call(
+    squares, grad_near, mom_near, freq_rows, stacked_near = pl.pallas_call(
         square_kernel,
-        in_specs=[hbm] * 2,
-        out_specs=[hbm, vmem, vmem],
+        in_specs=[hbm] * 4,
+        out_specs=[hbm] + [vmem] * 4,
         out_shape=[
-            pltpu.HBM((tensors, 8, LANES), F32),
+            pltpu.HBM((tensors, 1, LANES), F32),
             pltpu.VMEM(grad.shape, BF16),
+            pltpu.VMEM(mom.shape, F32),
             pltpu.VMEM((chunks, LANES), jnp.int32),
+            pltpu.VMEM(stacked.shape, BF16),
         ],
         scratch_shapes=[
             pltpu.VMEM(freq.shape, jnp.int32),
-            pltpu.VMEM((tensors, 8, LANES), F32),
-            pltpu.SemaphoreType.DMA((2,)),
+            pltpu.VMEM((tensors, 1, LANES), F32),
+            pltpu.SemaphoreType.DMA((4,)),
             pltpu.SemaphoreType.DMA((4,)),
         ],
         compiler_params=limit,
-    )(far(grad), far(freq))
+    )(far(grad), far(mom), far(freq), far(stacked))
     squares = spread(squares, "tensor", 2)
 
     kept, message = pl.pallas_call(
         kept_kernel,
-        in_specs=[scalar, hbm, vmem, vmem, vmem],
+        in_specs=[scalar] + [vmem] * 4,
         out_specs=[vmem, hbm],
         out_shape=[
             pltpu.VMEM((3 * chunks, LANES), F32),
             pltpu.HBM((replicas, 3 * chunks + 8, LANES), F32),
         ],
         scratch_shapes=[
-            pltpu.VMEM((4,) + TILE, F32),
             pltpu.VMEM((2, 2 * GROUP, 16 * LANES), BF16),
-            pltpu.SemaphoreType.DMA((1, 4)),
             pltpu.SemaphoreType.DMA((replicas,)),
         ],
         compiler_params=limit,
         cost_estimate=pl.CostEstimate(flops=2 * 10 ** 9, bytes_accessed=3 * 2 ** 20, transcendentals=0),
-    )(clip_flag, far(mom), near(grad_near), near(freq_rows), near(stacked))
+    )(clip_flag, near(mom_near), near(grad_near), near(freq_rows), near(stacked_near))
 
     message = pl.pallas_call(
         message_kernel,

time: 46.9 us -> 46 us (0.981)
  waiting for transfers between devices: 5.45 us -> 6.24 us
  local copies, waits for them, and re-layouts: 0.77 us -> 0.02 us
  Pallas kernels: 20.6 us -> 19.9 us
    all_to_all x2, waiting for transfers between devices: 5.45 us -> 6.24 us  [spread(): return lax.all_to_all(copies, axis, 0, 0, axis_index_groups=[order])]
    unnamed x8 -> x6, local copies, waits for them, and re-layouts: 0.77 us -> 0.02 us
    pallas_call x2, Pallas kernels: 6.08 us -> 5.34 us  [the longest x1 3.3 us: body(): pl.pallas_call(kept_kernel, in_specs=[scalar] + [vmem] * 4, out_specs=[vm...]
  transfers between devices with their start and end apart: 2 -> 2, of which waited for: 1 -> 2; matrix products, arithmetic and copies ran while one was open for 0% -> 0% of each run, Pallas kernels for 20% -> 18%
where the time goes in v7:
time: 46 us; the launch traced here: 45.8 us
  Pallas kernels  19.9 us (43%)
  starting transfers between devices  18.3 us (40%)
  waiting for transfers between devices  6.24 us (14%)
  between operations  1.34 us (3%)
    all_to_all x2, starting transfers between devices, spread(): return lax.all_to_all(copies, axis, 0, 0, axis_index_groups=[order])  18.3 us
    pallas_call x1, Pallas kernels, body(): pl.pallas_call(lambda *refs: update_kernel(replicas * tensors * rows * co...  8.59 us
    all_to_all x2, waiting for transfers between devices, spread(): return lax.all_to_all(copies, axis, 0, 0, axis_index_groups=[order])  6.24 us
    pallas_call x1, Pallas kernels, body(): pl.pallas_call(own_kernel, in_specs=[scalar, hbm, hbm, vmem, vmem], out_s...  5.12 us
    pallas_call x1, Pallas kernels, body(): pl.pallas_call(kept_kernel, in_specs=[scalar] + [vmem] * 4, out_specs=[vm...  3.3 us
    pallas_call x1, Pallas kernels, body(): pl.pallas_call(square_kernel, in_specs=[hbm] * 4, out_specs=[hbm] + [vmem...  2.04 us
  transfers between devices with their start and end apart: 2, of which 2 were waited for; matrix products, arithmetic and copies ran while one was open for 0% of the time, Pallas kernels for 18%

profile of v7, /device:TPU:1, one launch (start us, length us, event | category | flops | bytes accessed | tf_op | source)
XLA Modules:
  0.0 45.8 jit_solution(8384435624637894691)
XLA Ops:
  0.6 2.0 %shard_map.86 = (f32[16,1,128]{2,1,0:T(1,128)}, bf16[1024,512]{1,0:T(8,128)(2,1)S(1)}, f32[1024,512]{1,0:T(8,128)S(1)}, s32[32,128]{1,0:T(8,128)S(1)}, bf16[128,64]{1,0:T(8,128)(2,1)S(1)}) custom-call(bf16[1024,512]{1,0:T(8,128)(2,1)} %bitcast.6, f32[1024,512]{1,0:T(8,128)} %bitcast.4, s32[16,8,32]{2,1,0:T(8,128)} %bitcast.8, ...), custom_call_target="tpu_custom_call" | custom-call | tf_op jit(solution)/shard_map/pallas_call | solution.py:354
  2.7 9.9 %all-to-all-start = ((f32[16,1,128]{2,1,0:T(1,128)}), f32[16,1,128]{2,1,0:T(1,128)S(1)}, u32[]{:S(2)}, u32[]{:S(2)}) async-start(f32[16,1,128]{2,1,0:T(1,128)} %get-tuple-element.18), calls=%async_computation | async-start | bytes 16384 | tf_op jit(solution)/shard_map/all_to_all | solution.py:338
  13.2 3.3 %shard_map.87 = (f32[96,128]{1,0:T(8,128)S(1)}, f32[16,104,128]{2,1,0:T(8,128)}) custom-call(s32[1]{0:T(128)S(6)} %copy.11.flag_ref, f32[1024,512]{1,0:T(8,128)S(1)} %get-tuple-element.13.mom_ref, bf16[1024,512]{1,0:T(8,128)(2,1)S(1)} %get-tuple-element.14.grad_ref, s32[32,128]{1,0:T(8,128)S(1)} %get-tuple-element.15.freq_rows, ...), custom_call_target="tpu_custom_call" | custom-call | flops 2000000000 | bytes 3145728 | tf_op jit(solution)/shard_map/pallas_call | solution.py:375
  16.5 0.0 copy-start.2
  16.5 0.7 %all-to-all-done.square_ref = f32[16,1,128]{2,1,0:T(1,128)S(1)} async-done(((f32[16,1,128]{2,1,0:T(1,128)}), f32[16,1,128]{2,1,0:T(1,128)S(1)}, u32[]{:S(2)}, u32[]{:S(2)}) %all-to-all-start) | async-done | bytes 8224 | tf_op jit(solution)/shard_map/all_to_all | solution.py:338
  17.3 0.8 %shard_map.88 = f32[16,104,128]{2,1,0:T(8,128)} custom-call(f32[16,104,128]{2,1,0:T(8,128)} %get-tuple-element.17.message_hbm, f32[16,1,128]{2,1,0:T(1,128)S(1)} %all-to-all-done.square_ref), custom_call_target="tpu_custom_call", output_to_operand_aliasing={{}: (0, {})} | custom-call | tf_op jit(solution)/shard_map/pallas_call | solution.py:391
  18.1 8.4 %all-to-all-start.1 = ((f32[16,104,128]{2,1,0:T(8,128)}), f32[16,104,128]{2,1,0:T(8,128)S(1)}, u32[]{:S(2)}, u32[]{:S(2)}) async-start(f32[16,104,128]{2,1,0:T(8,128)} %shard_map.88), calls=%async_computation.1 | async-start | bytes 1703936 | tf_op jit(solution)/shard_map/all_to_all | solution.py:338
  26.5 0.0 copy-done.2
  26.5 0.0 copy-start
  26.5 0.0 copy-start.1
  26.6 5.1 %shard_map.89 = (f32[1024,512]{1,0:T(8,128)}, f32[1024,512]{1,0:T(8,128)}) custom-call(s32[1]{0:T(128)S(6)} %copy.11.flag_ref, f32[1024,512]{1,0:T(8,128)} %bitcast.5, bf16[1024,512]{1,0:T(8,128)(2,1)} %bitcast.7, f32[96,128]{1,0:T(8,128)S(1)} %get-tuple-element.19.kept_ref, bf16[128,64]{1,0:T(8,128)(2,1)S(1)} %copy-done.2), custom_call_target="tpu_custom_call" | custom-call | flops 2000000000 | bytes 7340032 | tf_op jit(solution)/shard_map/pallas_call | solution.py:402
  31.7 5.5 %all-to-all-done.1.refs_0_ = f32[16,104,128]{2,1,0:T(8,128)S(1)} async-done(((f32[16,104,128]{2,1,0:T(8,128)}), f32[16,104,128]{2,1,0:T(8,128)S(1)}, u32[]{:S(2)}, u32[]{:S(2)}) %all-to-all-start.1) | async-done | bytes 852000 | tf_op jit(solution)/shard_map/all_to_all | solution.py:338
  37.2 0.0 copy-done
  37.2 0.0 copy-done.1
  37.2 8.6 %shard_map.90 = (f32[1024,512]{1,0:T(8,128)}, f32[1024,512]{1,0:T(8,128)}) custom-call(f32[16,104,128]{2,1,0:T(8,128)S(1)} %all-to-all-done.1.refs_0_, f32[1024,512]{1,0:T(8,128)} %get-tuple-element.20.refs_1_, f32[1024,512]{1,0:T(8,128)} %get-tuple-element.21.refs_2_, bf16[256,256]{1,0:T(8,128)(2,1)S(1)} %copy-done.1, bf16[256,256]{1,0:T(8,128)(2,1)S(1)} %copy-done), custom_call_target="tpu_custom_call" | custom-call | tf_op jit(solution)/shard_map/pallas_call | solution.py:412
Async XLA Ops:
  2.7 14.6 %all-to-all-start = ((f32[16,1,128]{2,1,0:T(1,128)}), f32[16,1,128]{2,1,0:T(1,128)S(1)}, u32[]{:S(2)}, u32[]{:S(2)}) async-start(f32[16,1,128]{2,1,0:T(1,128)} %get-tuple-element.18), calls=%async_computation | async-start | bytes 16384 | tf_op jit(solution)/shard_map/all_to_all | solution.py:338
  16.5 10.0 %copy-start.2 = (bf16[128,64]{1,0:T(8,128)(2,1)S(1)}, bf16[128,64]{1,0:T(8,128)(2,1)}, u32[]{:S(2)}) copy-start(bf16[128,64]{1,0:T(8,128)(2,1)} %constant.6.clone.stacked_hbm.stacked_ref) | copy-start | bytes 49156
  18.1 19.1 %all-to-all-start.1 = ((f32[16,104,128]{2,1,0:T(8,128)}), f32[16,104,128]{2,1,0:T(8,128)S(1)}, u32[]{:S(2)}, u32[]{:S(2)}) async-start(f32[16,104,128]{2,1,0:T(8,128)} %shard_map.88), calls=%async_computation.1 | async-start | bytes 1703936 | tf_op jit(solution)/shard_map/all_to_all | solution.py:338
  26.5 10.7 %copy-start = (bf16[256,256]{1,0:T(8,128)(2,1)S(1)}, bf16[256,256]{1,0:T(8,128)(2,1)}, u32[]{:S(2)}) copy-start(bf16[256,256]{1,0:T(8,128)(2,1)} %constant.8.clone.refs_4_) | copy-start | bytes 393220
  26.5 10.7 %copy-start.1 = (bf16[256,256]{1,0:T(8,128)(2,1)S(1)}, bf16[256,256]{1,0:T(8,128)(2,1)}, u32[]{:S(2)}) copy-start(bf16[256,256]{1,0:T(8,128)(2,1)} %constant.7.clone.refs_3_) | copy-start | bytes 393220

commit v8 on v7

--- a/solution.py
+++ b/solution.py
@@ -121,7 +121,7 @@
     return out
 
 
-def kept_kernel(flag_ref, mom_ref, grad_ref, freq_rows, stacked_ref, out_ref, message_hbm, table, out_sems):
+def kept_kernel(flag_ref, mom_ref, grad_ref, freq_rows, stacked_ref, out_ref, message_hbm, table, packed, out_sems):
     flag = (flag_ref[0] == 1).astype(F32)
     stacked = stacked_ref[...]
     chunks = freq_rows.shape[0]
@@ -152,8 +152,9 @@
         return carry
 
     lax.fori_loop(0, 4, one, 0)
+    packed[:, 0, :] = out_ref[...]
     copies = [
-        pltpu.make_async_copy(out_ref, message_hbm.at[n, pl.ds(0, 3 * chunks)], out_sems.at[n])
+        pltpu.make_async_copy(packed, message_hbm.at[n, pl.ds(0, 3 * chunks)], out_sems.at[n])
         for n in range(message_hbm.shape[0])
     ]
     for copy in copies:
@@ -163,10 +164,9 @@
 
 
 def message_kernel(message_hbm, square_ref, out_hbm, total, sems):
-    total[...] = jnp.zeros_like(total)
-    total[:1, :] = jnp.sum(square_ref[...], axis=0)
+    total[...] = jnp.sum(square_ref[...], axis=0, keepdims=True)
     replicas, rows = out_hbm.shape[:2]
-    copies = [pltpu.make_async_copy(total, out_hbm.at[n, pl.ds(rows - 8, 8)], sems.at[n]) for n in range(replicas)]
+    copies = [pltpu.make_async_copy(total, out_hbm.at[n, pl.ds(rows - 1, 1)], sems.at[n]) for n in range(replicas)]
     for copy in copies:
         copy.start()
     for copy in copies:
@@ -218,9 +218,8 @@
         for copy in tile_copies(tile, inward, in_sems):
             copy.start()
     replicas = all_ref.shape[0]
-    chunks = (all_ref.shape[1] - 8) // 3
-    total = jnp.sum(all_ref[:, 3 * chunks:, :], axis=0)
-    total = jnp.sum(total, axis=(0, 1), keepdims=True)
+    chunks = (all_ref.shape[1] - 1) // 3
+    total = jnp.sum(all_ref[:, 3 * chunks, 0, :], axis=(0, 1), keepdims=True)
     rms = jnp.sqrt(total * (1.0 / count))
     factor = jnp.minimum(jnp.float32(1.0), CLIP_RMS / (rms + 1e-06))
     lane = lax.broadcasted_iota(jnp.int32, (8, LANES), 1) // TOPK
@@ -238,10 +237,10 @@
         for group in range(replicas // 4):
             ks, fs = [], []
             for r in range(4 * group, 4 * group + 4):
-                u = all_ref[r, pl.ds(at, 8), :]
-                v = all_ref[r, pl.ds(chunks + at, 8), :]
+                u = all_ref[r, pl.ds(at, 8), 0, :]
+                v = all_ref[r, pl.ds(chunks + at, 8), 0, :]
                 ks.append((u + factor * v) * (1.0 / replicas))
-                fs.append(all_ref[r, pl.ds(2 * chunks + at, 8), :])
+                fs.append(all_ref[r, pl.ds(2 * chunks + at, 8), 0, :])
             for m in range(4):
                 k = regroup(ks, m)
                 f = regroup(fs, m)
@@ -378,10 +377,11 @@
         out_specs=[vmem, hbm],
         out_shape=[
             pltpu.VMEM((3 * chunks, LANES), F32),
-            pltpu.HBM((replicas, 3 * chunks + 8, LANES), F32),
+            pltpu.HBM((replicas, 3 * chunks + 1, 1, LANES), F32),
         ],
         scratch_shapes=[
             pltpu.VMEM((2, 2 * GROUP, 16 * LANES), BF16),
+            pltpu.VMEM((3 * chunks, 1, LANES), F32),
             pltpu.SemaphoreType.DMA((replicas,)),
         ],
         compiler_params=limit,
@@ -394,7 +394,7 @@
         out_specs=hbm,
         out_shape=pltpu.HBM(message.shape, F32),
         input_output_aliases={0: 0},
-        scratch_shapes=[pltpu.VMEM((8, LANES), F32), pltpu.SemaphoreType.DMA((replicas,))],
+        scratch_shapes=[pltpu.VMEM((1, 1, LANES), F32), pltpu.SemaphoreType.DMA((replicas,))],
         compiler_params=limit,
     )(far(message), near(squares))
     everyone = spread(message, "replica", 4)

time: 46 us -> 45.6 us (level)
  waiting for transfers between devices: 6.24 us -> 5.47 us
    all_to_all x2, waiting for transfers between devices: 6.24 us -> 5.47 us  [spread(): return lax.all_to_all(copies, axis, 0, 0, axis_index_groups=[order])]
  transfers between devices with their start and end apart: 2 -> 2, of which waited for: 2 -> 2; matrix products, arithmetic and copies ran while one was open for 0% -> 0% of each run, Pallas kernels for 18% -> 19%
where the time goes in v8:
time: 45.6 us; the launch traced here: 45.4 us
  Pallas kernels  20.2 us (44%)
  starting transfers between devices  18.3 us (40%)
  waiting for transfers between devices  5.47 us (12%)
  between operations  1.34 us (3%)
    all_to_all x2, starting transfers between devices, spread(): return lax.all_to_all(copies, axis, 0, 0, axis_index_groups=[order])  18.3 us
    pallas_call x1, Pallas kernels, body(): pl.pallas_call(lambda *refs: update_kernel(replicas * tensors * rows * co...  8.88 us
    all_to_all x2, waiting for transfers between devices, spread(): return lax.all_to_all(copies, axis, 0, 0, axis_index_groups=[order])  5.47 us
    pallas_call x1, Pallas kernels, body(): pl.pallas_call(own_kernel, in_specs=[scalar, hbm, hbm, vmem, vmem], out_s...  5.12 us
    pallas_call x1, Pallas kernels, body(): pl.pallas_call(kept_kernel, in_specs=[scalar] + [vmem] * 4, out_specs=[vm...  3.45 us
    pallas_call x1, Pallas kernels, body(): pl.pallas_call(square_kernel, in_specs=[hbm] * 4, out_specs=[hbm] + [vmem...  2.04 us
  transfers between devices with their start and end apart: 2, of which 2 were waited for; matrix products, arithmetic and copies ran while one was open for 0% of the time, Pallas kernels for 19%

profile of v8, /device:TPU:1, one launch (start us, length us, event | category | flops | bytes accessed | tf_op | source)
XLA Modules:
  0.0 45.4 jit_solution(18432141517467493727)
XLA Ops:
  0.6 2.0 %shard_map.86 = (f32[16,1,128]{2,1,0:T(1,128)}, bf16[1024,512]{1,0:T(8,128)(2,1)S(1)}, f32[1024,512]{1,0:T(8,128)S(1)}, s32[32,128]{1,0:T(8,128)S(1)}, bf16[128,64]{1,0:T(8,128)(2,1)S(1)}) custom-call(bf16[1024,512]{1,0:T(8,128)(2,1)} %bitcast.6, f32[1024,512]{1,0:T(8,128)} %bitcast.4, s32[16,8,32]{2,1,0:T(8,128)} %bitcast.8, ...), custom_call_target="tpu_custom_call" | custom-call | tf_op jit(solution)/shard_map/pallas_call | solution.py:353
  2.7 9.9 %all-to-all-start = ((f32[16,1,128]{2,1,0:T(1,128)}), f32[16,1,128]{2,1,0:T(1,128)S(1)}, u32[]{:S(2)}, u32[]{:S(2)}) async-start(f32[16,1,128]{2,1,0:T(1,128)} %get-tuple-element.18), calls=%async_computation | async-start | bytes 16384 | tf_op jit(solution)/shard_map/all_to_all | solution.py:337
  13.2 3.5 %shard_map.87 = (f32[96,128]{1,0:T(8,128)S(1)}, f32[16,97,1,128]{3,2,1,0:T(1,128)}) custom-call(s32[1]{0:T(128)S(6)} %copy.11.flag_ref, f32[1024,512]{1,0:T(8,128)S(1)} %get-tuple-element.13.mom_ref, bf16[1024,512]{1,0:T(8,128)(2,1)S(1)} %get-tuple-element.14.grad_ref, s32[32,128]{1,0:T(8,128)S(1)} %get-tuple-element.15.freq_rows, ...), custom_call_target="tpu_custom_call" | custom-call | flops 2000000000 | bytes 3145728 | tf_op jit(solution)/shard_map/pallas_call | solution.py:374
  16.7 0.0 copy-start.2
  16.7 0.6 %all-to-all-done.square_ref = f32[16,1,128]{2,1,0:T(1,128)S(1)} async-done(((f32[16,1,128]{2,1,0:T(1,128)}), f32[16,1,128]{2,1,0:T(1,128)S(1)}, u32[]{:S(2)}, u32[]{:S(2)}) %all-to-all-start) | async-done | bytes 8224 | tf_op jit(solution)/shard_map/all_to_all | solution.py:337
  17.3 0.7 %shard_map.88 = f32[16,97,1,128]{3,2,1,0:T(1,128)} custom-call(f32[16,97,1,128]{3,2,1,0:T(1,128)} %get-tuple-element.17.message_hbm, f32[16,1,128]{2,1,0:T(1,128)S(1)} %all-to-all-done.square_ref), custom_call_target="tpu_custom_call", output_to_operand_aliasing={{}: (0, {})} | custom-call | tf_op jit(solution)/shard_map/pallas_call | solution.py:391
  18.0 8.4 %all-to-all-start.1 = ((f32[16,97,1,128]{3,2,1,0:T(1,128)}), f32[16,97,1,128]{3,2,1,0:T(1,128)S(1)}, u32[]{:S(2)}, u32[]{:S(2)}) async-start(f32[16,97,1,128]{3,2,1,0:T(1,128)} %shard_map.88), calls=%async_computation.1 | async-start | bytes 1589248 | tf_op jit(solution)/shard_map/all_to_all | solution.py:337
  26.4 0.0 copy-done.2
  26.4 0.0 copy-start
  26.5 0.0 copy-start.1
  26.5 5.1 %shard_map.89 = (f32[1024,512]{1,0:T(8,128)}, f32[1024,512]{1,0:T(8,128)}) custom-call(s32[1]{0:T(128)S(6)} %copy.11.flag_ref, f32[1024,512]{1,0:T(8,128)} %bitcast.5, bf16[1024,512]{1,0:T(8,128)(2,1)} %bitcast.7, f32[96,128]{1,0:T(8,128)S(1)} %get-tuple-element.19.kept_ref, bf16[128,64]{1,0:T(8,128)(2,1)S(1)} %copy-done.2), custom_call_target="tpu_custom_call" | custom-call | flops 2000000000 | bytes 7340032 | tf_op jit(solution)/shard_map/pallas_call | solution.py:402
  31.6 4.9 %all-to-all-done.1.refs_0_ = f32[16,97,1,128]{3,2,1,0:T(1,128)S(1)} async-done(((f32[16,97,1,128]{3,2,1,0:T(1,128)}), f32[16,97,1,128]{3,2,1,0:T(1,128)S(1)}, u32[]{:S(2)}, u32[]{:S(2)}) %all-to-all-start.1) | async-done | bytes 794656 | tf_op jit(solution)/shard_map/all_to_all | solution.py:337
  36.5 0.0 copy-done
  36.5 0.0 copy-done.1
  36.5 8.9 %shard_map.90 = (f32[1024,512]{1,0:T(8,128)}, f32[1024,512]{1,0:T(8,128)}) custom-call(f32[16,97,1,128]{3,2,1,0:T(1,128)S(1)} %all-to-all-done.1.refs_0_, f32[1024,512]{1,0:T(8,128)} %get-tuple-element.20.refs_1_, f32[1024,512]{1,0:T(8,128)} %get-tuple-element.21.refs_2_, bf16[256,256]{1,0:T(8,128)(2,1)S(1)} %copy-done.1, bf16[256,256]{1,0:T(8,128)(2,1)S(1)} %copy-done), custom_call_target="tpu_custom_call" | custom-call | tf_op jit(solution)/shard_map/pallas_call | solution.py:412
Async XLA Ops:
  2.7 14.6 %all-to-all-start = ((f32[16,1,128]{2,1,0:T(1,128)}), f32[16,1,128]{2,1,0:T(1,128)S(1)}, u32[]{:S(2)}, u32[]{:S(2)}) async-start(f32[16,1,128]{2,1,0:T(1,128)} %get-tuple-element.18), calls=%async_computation | async-start | bytes 16384 | tf_op jit(solution)/shard_map/all_to_all | solution.py:337
  16.7 9.8 %copy-start.2 = (bf16[128,64]{1,0:T(8,128)(2,1)S(1)}, bf16[128,64]{1,0:T(8,128)(2,1)}, u32[]{:S(2)}) copy-start(bf16[128,64]{1,0:T(8,128)(2,1)} %constant.6.clone.stacked_hbm.stacked_ref) | copy-start | bytes 49156
  18.0 18.5 %all-to-all-start.1 = ((f32[16,97,1,128]{3,2,1,0:T(1,128)}), f32[16,97,1,128]{3,2,1,0:T(1,128)S(1)}, u32[]{:S(2)}, u32[]{:S(2)}) async-start(f32[16,97,1,128]{3,2,1,0:T(1,128)} %shard_map.88), calls=%async_computation.1 | async-start | bytes 1589248 | tf_op jit(solution)/shard_map/all_to_all | solution.py:337
  26.4 10.1 %copy-start = (bf16[256,256]{1,0:T(8,128)(2,1)S(1)}, bf16[256,256]{1,0:T(8,128)(2,1)}, u32[]{:S(2)}) copy-start(bf16[256,256]{1,0:T(8,128)(2,1)} %constant.8.clone.refs_4_) | copy-start | bytes 393220
  26.5 10.0 %copy-start.1 = (bf16[256,256]{1,0:T(8,128)(2,1)S(1)}, bf16[256,256]{1,0:T(8,128)(2,1)}, u32[]{:S(2)}) copy-start(bf16[256,256]{1,0:T(8,128)(2,1)} %constant.7.clone.refs_3_) | copy-start | bytes 393220

commit v9 on v8

--- a/solution.py
+++ b/solution.py
@@ -163,14 +163,14 @@
         copy.wait()
 
 
-def message_kernel(message_hbm, square_ref, out_hbm, total, sems):
-    total[...] = jnp.sum(square_ref[...], axis=0, keepdims=True)
+def message_kernel(message_hbm, square_ref, out_hbm, total, sem):
     replicas, rows = out_hbm.shape[:2]
-    copies = [pltpu.make_async_copy(total, out_hbm.at[n, pl.ds(rows - 1, 1)], sems.at[n]) for n in range(replicas)]
-    for copy in copies:
-        copy.start()
-    for copy in copies:
-        copy.wait()
+    line = jnp.sum(square_ref[...], axis=0, keepdims=True)
+    for n in range(replicas):
+        total[n] = line
+    copy = pltpu.make_async_copy(total, out_hbm.at[:, pl.ds(rows - 1, 1)], sem)
+    copy.start()
+    copy.wait()
 
 
 def own_kernel(flag_ref, mom_hbm, grad_hbm, kept_ref, stacked_ref, u_hbm, v_hbm, mom, grad, u_out, v_out, in_sems, out_sems):
@@ -394,7 +394,7 @@
         out_specs=hbm,
         out_shape=pltpu.HBM(message.shape, F32),
         input_output_aliases={0: 0},
-        scratch_shapes=[pltpu.VMEM((1, 1, LANES), F32), pltpu.SemaphoreType.DMA((replicas,))],
+        scratch_shapes=[pltpu.VMEM((replicas, 1, 1, LANES), F32), pltpu.SemaphoreType.DMA],
         compiler_params=limit,
     )(far(message), near(squares))
     everyone = spread(message, "replica", 4)

time: 45.6 us -> 45.5 us (level)
  no operation moved by 1% of the time
where the time goes in v9:
time: 45.5 us; the launch traced here: 45.3 us
  Pallas kernels  20.1 us (44%)
  starting transfers between devices  18.3 us (40%)
  waiting for transfers between devices  5.48 us (12%)
  between operations  1.34 us (3%)
    all_to_all x2, starting transfers between devices, spread(): return lax.all_to_all(copies, axis, 0, 0, axis_index_groups=[order])  18.3 us
    pallas_call x1, Pallas kernels, body(): pl.pallas_call(lambda *refs: update_kernel(replicas * tensors * rows * co...  8.88 us
    all_to_all x2, waiting for transfers between devices, spread(): return lax.all_to_all(copies, axis, 0, 0, axis_index_groups=[order])  5.48 us
    pallas_call x1, Pallas kernels, body(): pl.pallas_call(own_kernel, in_specs=[scalar, hbm, hbm, vmem, vmem], out_s...  5.12 us
    pallas_call x1, Pallas kernels, body(): pl.pallas_call(kept_kernel, in_specs=[scalar] + [vmem] * 4, out_specs=[vm...  3.45 us
    pallas_call x1, Pallas kernels, body(): pl.pallas_call(square_kernel, in_specs=[hbm] * 4, out_specs=[hbm] + [vmem...  2.04 us
  transfers between devices with their start and end apart: 2, of which 2 were waited for; matrix products, arithmetic and copies ran while one was open for 0% of the time, Pallas kernels for 19%

profile of v9, /device:TPU:1, one launch (start us, length us, event | category | flops | bytes accessed | tf_op | source)
XLA Modules:
  0.0 45.3 jit_solution(8534452852938875093)
XLA Ops:
  0.6 2.0 %shard_map.86 = (f32[16,1,128]{2,1,0:T(1,128)}, bf16[1024,512]{1,0:T(8,128)(2,1)S(1)}, f32[1024,512]{1,0:T(8,128)S(1)}, s32[32,128]{1,0:T(8,128)S(1)}, bf16[128,64]{1,0:T(8,128)(2,1)S(1)}) custom-call(bf16[1024,512]{1,0:T(8,128)(2,1)} %bitcast.6, f32[1024,512]{1,0:T(8,128)} %bitcast.4, s32[16,8,32]{2,1,0:T(8,128)} %bitcast.8, ...), custom_call_target="tpu_custom_call" | custom-call | tf_op jit(solution)/shard_map/pallas_call | solution.py:353
  2.7 9.9 %all-to-all-start = ((f32[16,1,128]{2,1,0:T(1,128)}), f32[16,1,128]{2,1,0:T(1,128)S(1)}, u32[]{:S(2)}, u32[]{:S(2)}) async-start(f32[16,1,128]{2,1,0:T(1,128)} %get-tuple-element.18), calls=%async_computation | async-start | bytes 16384 | tf_op jit(solution)/shard_map/all_to_all | solution.py:337
  13.2 3.5 %shard_map.87 = (f32[96,128]{1,0:T(8,128)S(1)}, f32[16,97,1,128]{3,2,1,0:T(1,128)}) custom-call(s32[1]{0:T(128)S(6)} %copy.11.flag_ref, f32[1024,512]{1,0:T(8,128)S(1)} %get-tuple-element.13.mom_ref, bf16[1024,512]{1,0:T(8,128)(2,1)S(1)} %get-tuple-element.14.grad_ref, s32[32,128]{1,0:T(8,128)S(1)} %get-tuple-element.15.freq_rows, ...), custom_call_target="tpu_custom_call" | custom-call | flops 2000000000 | bytes 3145728 | tf_op jit(solution)/shard_map/pallas_call | solution.py:374
  16.7 0.0 copy-start.2
  16.7 0.6 %all-to-all-done.square_ref = f32[16,1,128]{2,1,0:T(1,128)S(1)} async-done(((f32[16,1,128]{2,1,0:T(1,128)}), f32[16,1,128]{2,1,0:T(1,128)S(1)}, u32[]{:S(2)}, u32[]{:S(2)}) %all-to-all-start) | async-done | bytes 8224 | tf_op jit(solution)/shard_map/all_to_all | solution.py:337
  17.3 0.6 %shard_map.88 = f32[16,97,1,128]{3,2,1,0:T(1,128)} custom-call(f32[16,97,1,128]{3,2,1,0:T(1,128)} %get-tuple-element.17.message_hbm, f32[16,1,128]{2,1,0:T(1,128)S(1)} %all-to-all-done.square_ref), custom_call_target="tpu_custom_call", output_to_operand_aliasing={{}: (0, {})} | custom-call | tf_op jit(solution)/shard_map/pallas_call | solution.py:391
  17.9 8.4 %all-to-all-start.1 = ((f32[16,97,1,128]{3,2,1,0:T(1,128)}), f32[16,97,1,128]{3,2,1,0:T(1,128)S(1)}, u32[]{:S(2)}, u32[]{:S(2)}) async-start(f32[16,97,1,128]{3,2,1,0:T(1,128)} %shard_map.88), calls=%async_computation.1 | async-start | bytes 1589248 | tf_op jit(solution)/shard_map/all_to_all | solution.py:337
  26.3 0.0 copy-done.2
  26.3 0.0 copy-start
  26.4 0.0 copy-start.1
  26.4 5.1 %shard_map.89 = (f32[1024,512]{1,0:T(8,128)}, f32[1024,512]{1,0:T(8,128)}) custom-call(s32[1]{0:T(128)S(6)} %copy.11.flag_ref, f32[1024,512]{1,0:T(8,128)} %bitcast.5, bf16[1024,512]{1,0:T(8,128)(2,1)} %bitcast.7, f32[96,128]{1,0:T(8,128)S(1)} %get-tuple-element.19.kept_ref, bf16[128,64]{1,0:T(8,128)(2,1)S(1)} %copy-done.2), custom_call_target="tpu_custom_call" | custom-call | flops 2000000000 | bytes 7340032 | tf_op jit(solution)/shard_map/pallas_call | solution.py:402
  31.5 4.9 %all-to-all-done.1.refs_0_ = f32[16,97,1,128]{3,2,1,0:T(1,128)S(1)} async-done(((f32[16,97,1,128]{3,2,1,0:T(1,128)}), f32[16,97,1,128]{3,2,1,0:T(1,128)S(1)}, u32[]{:S(2)}, u32[]{:S(2)}) %all-to-all-start.1) | async-done | bytes 794656 | tf_op jit(solution)/shard_map/all_to_all | solution.py:337
  36.4 0.0 copy-done
  36.4 0.0 copy-done.1
  36.4 8.9 %shard_map.90 = (f32[1024,512]{1,0:T(8,128)}, f32[1024,512]{1,0:T(8,128)}) custom-call(f32[16,97,1,128]{3,2,1,0:T(1,128)S(1)} %all-to-all-done.1.refs_0_, f32[1024,512]{1,0:T(8,128)} %get-tuple-element.20.refs_1_, f32[1024,512]{1,0:T(8,128)} %get-tuple-element.21.refs_2_, bf16[256,256]{1,0:T(8,128)(2,1)S(1)} %copy-done.1, bf16[256,256]{1,0:T(8,128)(2,1)S(1)} %copy-done), custom_call_target="tpu_custom_call" | custom-call | tf_op jit(solution)/shard_map/pallas_call | solution.py:412
Async XLA Ops:
  2.7 14.6 %all-to-all-start = ((f32[16,1,128]{2,1,0:T(1,128)}), f32[16,1,128]{2,1,0:T(1,128)S(1)}, u32[]{:S(2)}, u32[]{:S(2)}) async-start(f32[16,1,128]{2,1,0:T(1,128)} %get-tuple-element.18), calls=%async_computation | async-start | bytes 16384 | tf_op jit(solution)/shard_map/all_to_all | solution.py:337
  16.7 9.7 %copy-start.2 = (bf16[128,64]{1,0:T(8,128)(2,1)S(1)}, bf16[128,64]{1,0:T(8,128)(2,1)}, u32[]{:S(2)}) copy-start(bf16[128,64]{1,0:T(8,128)(2,1)} %constant.6.clone.stacked_hbm.stacked_ref) | copy-start | bytes 49156
  17.9 18.5 %all-to-all-start.1 = ((f32[16,97,1,128]{3,2,1,0:T(1,128)}), f32[16,97,1,128]{3,2,1,0:T(1,128)S(1)}, u32[]{:S(2)}, u32[]{:S(2)}) async-start(f32[16,97,1,128]{3,2,1,0:T(1,128)} %shard_map.88), calls=%async_computation.1 | async-start | bytes 1589248 | tf_op jit(solution)/shard_map/all_to_all | solution.py:337
  26.3 10.1 %copy-start = (bf16[256,256]{1,0:T(8,128)(2,1)S(1)}, bf16[256,256]{1,0:T(8,128)(2,1)}, u32[]{:S(2)}) copy-start(bf16[256,256]{1,0:T(8,128)(2,1)} %constant.8.clone.refs_4_) | copy-start | bytes 393220
  26.4 10.0 %copy-start.1 = (bf16[256,256]{1,0:T(8,128)(2,1)S(1)}, bf16[256,256]{1,0:T(8,128)(2,1)}, u32[]{:S(2)}) copy-start(bf16[256,256]{1,0:T(8,128)(2,1)} %constant.7.clone.refs_3_) | copy-start | bytes 393220
